TPU v7x, 32 devices: a whole 2x2x4 slice. The times are simulated.
32 devices in a mesh: groups: 2 (over y), leaf: 4 (over z), state: 2 (over x), sub: 2 (over core).
Axes of the slice: x: 2, y: 2, z: 4, core: 2. Of those that a mesh axis runs over, the one named last changes fastest.
Arguments:
- sphere_coef: bfloat16 [12, 25, 2, 2, 4, 2048], P(None, None, None, None, None, ('groups', 'leaf', 'state', 'sub')), parts along dimension 5, may hold values from -6 to 6
- live_blocks: int32 [32], P(('groups', 'leaf', 'state', 'sub')), parts along dimension 0, may hold values from 1 to 4, as said below
- cluster: int32 [2048], P(('groups', 'leaf', 'state', 'sub')), parts along dimension 0, may hold values from 0 to 15
- leaf_parent: int32 [512], P(('groups', 'leaf', 'state', 'sub')), parts along dimension 0, may hold values from 0 to 1
- leaf_octant: int32 [512], P(('groups', 'leaf', 'state', 'sub')), parts along dimension 0, may hold values from 0 to 7
- box_octant: int32 [64], P(('groups', 'leaf', 'state', 'sub')), parts along dimension 0, may hold values from 0 to 7
- rotation: float32 [8, 2, 12, 25, 25], replicated, may hold values from -0.875 to 0.875
- axial_one: float32 [2, 25, 2, 12, 2, 12], replicated, may hold values from -0.3125 to 0.3125
- axial_two: float32 [2, 25, 2, 12, 2, 12], replicated, may hold values from -0.3125 to 0.3125
- owner_rotation: float32 [8, 2, 12, 25, 25], P(('groups', 'leaf')), parts along dimension 0, may hold values from -0.875 to 0.875
- owner_axial: float32 [8, 2, 25, 2, 128, 2, 12], P(('groups', 'leaf'), None, None, None, ('state', 'sub')), parts along dimension 0, may hold values from -0.875 to 0.875
- owner_angle: float32 [8], P('groups'), parts along dimension 0, may hold values from -3.140625 to 3.140625
- turn_table: bfloat16 [8, 128, 25, 256], P(('groups', 'leaf'), ('state', 'sub')), parts along dimension 0, may hold values from -0.625 to 0.625
- angular_table: bfloat16 [256, 128, 32], P('leaf', ('state', 'sub')), may hold values from -0.375 to 0.375
Outputs:
- far_field: float32 [32, 4, 2, 2, 2048], P(('groups', 'leaf', 'state', 'sub')), parts along dimension 0
There are 2 independent parts, one for each index of `groups`. A program takes and returns all parts, laid end to end along the dimension named above; an argument that names none is the same for every part. Nothing has to cross between parts.
Inputs may be any that keep to these rules, and one draw needn't show every extreme that they name: `live_blocks`: live blocks of 16 sphere slots on each device; some device has all 4 live in every draw.
All inputs are finite; a program needn't handle non-finite values.
Results may differ from a plain program's by a relative error of at most 0.018.
Values may be sent and summed in bfloat16 or wider, within the bound.
A program may use at most 64 MiB of HBM per device.

v0:
```python
import math

import jax
import jax.numpy as jnp
from jax import lax
from jax.sharding import PartitionSpec as P

STATES = 4
SBLK = 4
PHI = 2048


def complex_join(first, second, half):
    real = first[..., :half] - second[..., half:]
    imag = first[..., half:] + second[..., :half]
    return jnp.concatenate([real, imag], axis=-1)


def turn_select(vectors, rotation, octants, backward):
    degrees, orders, width = vectors.shape
    if backward:
        mats = jnp.transpose(rotation, (1, 2, 0, 4, 3))
        sign = -1.0
    else:
        mats = jnp.transpose(rotation, (1, 2, 0, 3, 4))
        sign = 1.0
    mats = mats.reshape(2, degrees, 8 * orders, orders)
    first = jnp.einsum("lQp,lpC->lQC", mats[0], vectors, precision=lax.Precision.HIGHEST)
    second = sign * jnp.einsum("lQp,lpC->lQC", mats[1], vectors, precision=lax.Precision.HIGHEST)
    joined = complex_join(first, second, width // 2).reshape(degrees, 8, orders, width)
    count = octants.shape[0]
    chosen = (octants[None, :] == jnp.arange(8, dtype=jnp.int32)[:, None]).astype(jnp.float32)
    column_mask = jnp.tile(chosen, (1, width // count))
    return jnp.sum(joined * column_mask[None, :, None, :], axis=1)


def axial_apply(vectors, axial):
    degrees, orders, width = vectors.shape
    rest = width // 4
    moved = vectors.reshape(degrees, orders, 2, 2, rest)
    moved = jnp.transpose(moved, (1, 3, 0, 2, 4)).reshape(orders, 2 * degrees, 2 * rest)
    mats = axial.reshape(2, orders, 2 * degrees, 2 * degrees)
    first = jnp.einsum("qab,qbC->qaC", mats[0], moved, precision=lax.Precision.HIGHEST)
    second = jnp.einsum("qab,qbC->qaC", mats[1], moved, precision=lax.Precision.HIGHEST)
    joined = complex_join(first, second, rest).reshape(orders, 2, degrees, 2, rest)
    return jnp.transpose(joined, (2, 0, 3, 1, 4)).reshape(degrees, orders, width)


def move_expansion(vectors, octants, rotation, axial):
    turned = turn_select(vectors, rotation, octants, False)
    return turn_select(axial_apply(turned, axial), rotation, octants, True)


def local_boxes(
    sphere_block,
    live_count,
    cluster,
    leaf_parent,
    leaf_octant,
    box_octant,
    rotation,
    axial_one,
    axial_two,
):
    degrees, orders = (sphere_block.shape[0], sphere_block.shape[1])
    channel = sphere_block.shape[2] * sphere_block.shape[3] * sphere_block.shape[4]
    slots = sphere_block.shape[-1]
    per_block = slots // SBLK
    alive = jnp.arange(slots, dtype=jnp.int32) // per_block < live_count
    leaf_total = leaf_parent.shape[0]
    member = (
        (cluster[:, None] == jnp.arange(leaf_total, dtype=jnp.int32)[None, :]) & alive[:, None]
    ).astype(jnp.bfloat16)
    ident = jnp.eye(channel, dtype=jnp.bfloat16)
    spread = (ident[:, None, :, None] * member[None, :, None, :]).reshape(
        channel * slots, channel * leaf_total
    )
    leaves = jnp.dot(
        sphere_block.reshape(degrees * orders, channel * slots),
        spread,
        preferred_element_type=jnp.float32,
    ).reshape(degrees, orders, channel * leaf_total)
    moved = move_expansion(leaves, leaf_octant, rotation, axial_one)
    box_total = box_octant.shape[0]
    parents = (leaf_parent[:, None] == jnp.arange(box_total, dtype=jnp.int32)[None, :]).astype(
        jnp.float32
    )
    wide_ident = jnp.eye(channel, dtype=jnp.float32)
    wide_parents = (wide_ident[:, None, :, None] * parents[None, :, None, :]).reshape(
        channel * leaf_total, channel * box_total
    )
    boxes = jnp.einsum("lpC,CD->lpD", moved, wide_parents, precision=lax.Precision.HIGHEST)
    outer = move_expansion(boxes, box_octant, rotation, axial_two)
    return outer.reshape(degrees, orders, channel, box_total).sum(-1)


def owner_frame(owner_sum, owner_turn, owner_shift):
    degrees, orders, width = owner_sum.shape
    states = width // 4
    first = jnp.einsum("lqp,lpC->lqC", owner_turn[0], owner_sum, precision=lax.Precision.HIGHEST)
    second = jnp.einsum("lqp,lpC->lqC", owner_turn[1], owner_sum, precision=lax.Precision.HIGHEST)
    turned = complex_join(first, second, width // 2)
    moved = turned.reshape(degrees, orders, 2, 2, states)
    moved = jnp.transpose(moved, (1, 3, 0, 2, 4)).reshape(orders, 2 * degrees, 2 * states)
    root_degrees = owner_shift.shape[3]
    mats = owner_shift.reshape(2, orders, 2 * root_degrees, 2 * degrees)
    first = jnp.einsum("qab,qbC->qaC", mats[0], moved, precision=lax.Precision.HIGHEST)
    second = jnp.einsum("qab,qbC->qaC", mats[1], moved, precision=lax.Precision.HIGHEST)
    joined = complex_join(first, second, states).reshape(orders, 2, root_degrees, 2, states)
    framed = jnp.transpose(joined, (2, 1, 3, 4, 0)).reshape(root_degrees, 4 * states, orders)
    return framed.astype(jnp.bfloat16)


def rotate_back(framed, functions, azimuth, half_orders):
    root_degrees, width = (framed.shape[0], framed.shape[1])
    states = width // 4
    orders_here = functions.shape[2]
    values = jnp.einsum("nCm,nmj->nCj", framed, functions, preferred_element_type=jnp.float32)
    values = values.reshape(root_degrees, 2, 2, states, orders_here)
    order_values = (jnp.arange(orders_here, dtype=jnp.int32) - half_orders).astype(jnp.float32)
    cosine = jnp.cos(order_values * azimuth)
    sine = jnp.sin(order_values * azimuth)
    real_part = cosine * values[:, :, 0] + sine * values[:, :, 1]
    imag_part = cosine * values[:, :, 1] - sine * values[:, :, 0]
    joined = jnp.stack([real_part, imag_part], axis=2)
    return jnp.transpose(joined, (4, 1, 2, 3, 0)).reshape(orders_here, 4 * states * root_degrees)


def legendre_field(root_coef, table):
    orders_here, root_degrees = (table.shape[0], table.shape[1])
    lat_total = table.shape[2] // 2
    rows = root_coef.shape[1] // root_degrees
    states = rows // 4
    half = rows // 2
    blocks = jnp.einsum(
        "jrn,jnK->jrK",
        root_coef.reshape(orders_here, rows, root_degrees),
        table,
        preferred_element_type=jnp.float32,
    )
    theta_part = blocks[:, :half, :lat_total] + blocks[:, half:, lat_total:]
    cross = blocks[:, :half, lat_total:] + blocks[:, half:, :lat_total]
    phi_part = jnp.concatenate([-cross[:, states:], cross[:, :states]], axis=1)
    return jnp.concatenate([theta_part, phi_part], axis=1)


def phase_table(orders, longitudes):
    order_ids = jnp.arange(orders, dtype=jnp.int32) - orders // 2
    column = jnp.arange(2 * longitudes, dtype=jnp.int32)
    along = column % longitudes
    quarter = (column // longitudes).astype(jnp.float32)
    remainder = jnp.mod(order_ids[:, None] * along[None, :], longitudes)
    phase = remainder.astype(jnp.float32) * (2.0 * math.pi / longitudes) - quarter[None, :] * (
        0.5 * math.pi
    )
    return jnp.cos(phase).astype(jnp.bfloat16)


def synthesize(spectrum, longitudes, states):
    orders = spectrum.shape[1]
    table = phase_table(orders, longitudes)
    product = jnp.dot(spectrum, table, preferred_element_type=jnp.float32)
    product = product.reshape(2, 2, states, -1, 2 * longitudes)
    real_part = product[:, 0, :, :, :longitudes] - product[:, 1, :, :, longitudes:]
    imag_part = product[:, 0, :, :, longitudes:] + product[:, 1, :, :, :longitudes]
    joined = jnp.stack([real_part, imag_part], axis=3)
    return jnp.transpose(joined, (2, 1, 0, 3, 4)) * (1.0 / math.sqrt(orders))


def on_device(
    sphere_coef,
    live_blocks,
    cluster,
    leaf_parent,
    leaf_octant,
    box_octant,
    rotation,
    axial_one,
    axial_two,
    owner_rotation,
    owner_axial,
    owner_angle,
    turn_table,
    angular_table,
):
    partial_owner = local_boxes(
        sphere_coef,
        live_blocks[0],
        cluster,
        leaf_parent,
        leaf_octant,
        box_octant,
        rotation,
        axial_one,
        axial_two,
    )
    owner_sum = lax.psum(partial_owner, ("state", "sub"))
    framed = owner_frame(owner_sum, owner_rotation[0], owner_axial[0])
    leaf_size = lax.axis_size("leaf")
    orders = turn_table.shape[3]
    half_orders = orders // 2
    own_orders = orders // leaf_size
    own_azimuth = owner_angle[lax.axis_index("leaf")]
    piece = turn_table[0]
    root = lax.psum_scatter(
        rotate_back(framed, piece, own_azimuth, half_orders),
        "leaf",
        scatter_dimension=0,
        tiled=True,
    )
    root_coef = root.astype(jnp.bfloat16)
    field = legendre_field(root_coef, angular_table)
    channel = field.shape[1]
    group_size = lax.axis_size("state") * lax.axis_size("sub")
    lat_rows = field.shape[2] // (leaf_size * group_size)
    shaped = field.reshape(own_orders, channel, leaf_size, group_size, lat_rows)
    shaped = jnp.transpose(shaped, (3, 2, 1, 4, 0)).reshape(
        group_size, leaf_size, channel * lat_rows * own_orders
    )
    summed = lax.psum_scatter(
        shaped.astype(jnp.bfloat16), ("state", "sub"), scatter_dimension=0, tiled=True
    )
    moved = lax.all_to_all(summed, "leaf", split_axis=1, concat_axis=2, tiled=True)
    spectrum = moved.reshape(leaf_size, channel, lat_rows, own_orders)
    spectrum = jnp.transpose(spectrum, (1, 2, 0, 3)).reshape(channel * lat_rows, orders)
    return synthesize(spectrum, PHI, STATES)


def solution(mesh):
    return jax.shard_map(
        on_device,
        mesh=mesh,
        in_specs=(
            P(None, None, None, None, None, ("groups", "leaf", "state", "sub")),
            P(("groups", "leaf", "state", "sub")),
            P(("groups", "leaf", "state", "sub")),
            P(("groups", "leaf", "state", "sub")),
            P(("groups", "leaf", "state", "sub")),
            P(("groups", "leaf", "state", "sub")),
            P(),
            P(),
            P(),
            P(("groups", "leaf"), None, None, None, None),
            P(("groups", "leaf"), None, None, None, ("state", "sub"), None, None),
            P("groups"),
            P(("groups", "leaf"), ("state", "sub"), None, None),
            P("leaf", ("state", "sub"), None),
        ),
        out_specs=P(("groups", "leaf", "state", "sub"), None, None, None, None),
        check_vma=False,
    )
```

profile of v0, /device:TPU:0, one launch (start us, length us, event | category | flops | bytes accessed | tf_op | source)
XLA Modules:
  0.0 170.0 jit_solution(8647744957523525391)
XLA Ops:
  6.5 0.6 fusion.33
  7.1 4.5 %fusion.46 = (f32[1,12,8,25,25]{4,0,3,1,2:T(1,128)S(1)}, f32[1,12,8,25,25]{4,0,3,1,2:T(1,128)S(1)}) fusion(f32[2,12,8,25,25]{4,0,3,1,2:T(2,128)} %bitcast.182), kind=kLoop, calls=%fused_computation.129 | loop fusion | bytes 960000 | tf_op jit(solution)/shard_map/slice | solution.py:28
  11.7 2.4 %copy.163 = f32[1,12,8,25,25]{3,2,4,1,0:T(8,128)} copy(f32[1,12,8,25,25]{4,0,3,1,2:T(1,128)S(1)} %get-tuple-element.12) | data formatting | bytes 480000 | tf_op jit(solution)/shard_map/slice | solution.py:29
  14.1 2.4 %squeeze.61 = f32[12,200,25]{1,2,0:T(8,128)} reshape(f32[1,12,8,25,25]{3,2,4,1,0:T(8,128)} %copy.163) | data formatting | bytes 480000 | tf_op jit(solution)/shard_map/squeeze | solution.py:29
  17.4 0.7 mul.178
  18.1 2.6 %reshape.344 = bf16[300,1024]{1,0:T(8,128)(2,1)S(1)} reshape(bf16[12,25,2,2,4,64]{5,4,3,2,1,0:T(4,128)(2,1)} %param.14) | data formatting | bytes 1228800 | tf_op jit(solution)/shard_map/reshape | solution.py:79
  21.2 1.1 copy.162
  22.7 3.3 %convolution_bitcast_fusion.2 = f32[12,200,256]{2,1,0:T(8,128)S(1)} fusion(f32[12,25,256]{2,1,0:T(8,128)S(1)} %reshape.345, f32[12,200,25]{1,2,0:T(8,128)} %squeeze.61), kind=kOutput, calls=%fused_computation.26 | convolution fusion | flops 184320000 | bytes 3004800 | tf_op jit(solution)/shard_map/lQp,lpC->lQC/dot_general | solution.py:29
  26.0 2.2 %convolution_bitcast_fusion.3 = f32[12,200,256]{2,1,0:T(8,128)S(1)} fusion(f32[12,25,256]{2,1,0:T(8,128)S(1)} %reshape.345, f32[12,200,25]{1,2,0:T(8,128)S(1)} %squeeze.60), kind=kOutput, calls=%fused_computation.27 | convolution fusion | flops 184320000 | bytes 3004800 | tf_op jit(solution)/shard_map/lQp,lpC->lQC/dot_general | solution.py:28
  28.4 1.6 pad_maximum_fusion
  30.1 2.5 %reshape.346 = f32[12,8,25,256]{3,2,1,0:T(8,128)S(1)} reshape(f32[12,200,256]{2,1,0:T(8,128)} %pad_maximum_fusion) | data formatting | bytes 4915200 | tf_op jit(solution)/shard_map/reshape | solution.py:30
  32.5 0.7 fusion.37
  33.2 0.6 tile.8
  33.8 1.5 tile.9
  35.4 1.9 %multiply_reduce_fusion.1 = f32[12,25,256]{2,1,0:T(8,128)} fusion(f32[12,8,25,256]{3,2,1,0:T(8,128)S(1)} %reshape.346, f32[8,256]{1,0:T(8,128)} %tile.9), kind=kLoop, calls=%fused_computation.13 | loop fusion | flops 1152000 | bytes 2772992 | tf_op jit(solution)/shard_map/reduce_sum | solution.py:34
  37.2 1.4 reshape.347
  39.4 0.7 copy.206
  40.4 1.1 copy.205
  41.8 0.6 convolution_bitcast_fusion.8
  42.5 0.6 convolution_bitcast_fusion.9
  43.5 1.2 reshape.349
  44.7 2.2 %copy.169 = f32[12,25,2,2,64]{4,3,2,1,0:T(2,128)} copy(f32[12,25,2,2,64]{4,2,0,3,1:T(2,128)} %bitcast.184) | data formatting | bytes 614400 | tf_op jit(solution)/shard_map/transpose | solution.py:46
  46.9 1.5 reshape.350
  48.4 2.9 %fusion.45 = (f32[1,12,8,25,25]{3,0,4,1,2:T(1,128)S(1)}, f32[1,12,8,25,25]{3,0,4,1,2:T(1,128)}) fusion(f32[2,12,8,25,25]{3,0,4,1,2:T(2,128)S(1)} %bitcast.183), kind=kLoop, calls=%fused_computation.128 | loop fusion | bytes 960000 | tf_op jit(solution)/shard_map/slice | solution.py:28
  51.5 1.1 squeeze.64
  53.1 3.3 %convolution_bitcast_fusion.1 = f32[12,200,256]{2,1,0:T(8,128)S(1)} fusion(f32[12,25,256]{2,1,0:T(8,128)S(1)} %reshape.350, f32[12,200,25]{1,2,0:T(8,128)} %squeeze.64), kind=kOutput, calls=%fused_computation.25 | convolution fusion | flops 184320000 | bytes 3004800 | tf_op jit(solution)/shard_map/lQp,lpC->lQC/dot_general | solution.py:28
  56.5 2.2 %multiply_bitcast_fusion = f32[12,200,256]{2,1,0:T(8,128)S(1)} fusion(f32[12,25,256]{2,1,0:T(8,128)S(1)} %reshape.350, f32[12,200,25]{1,2,0:T(8,128)S(1)} %squeeze.65), kind=kOutput, calls=%fused_computation.16 | convolution fusion | flops 184934400 | bytes 3004800 | tf_op jit(solution)/shard_map/lQp,lpC->lQC/dot_general | solution.py:29
  58.9 1.6 pad_maximum_fusion.1
  60.5 2.6 %reshape.351 = f32[12,8,25,256]{3,2,1,0:T(8,128)S(1)} reshape(f32[12,200,256]{2,1,0:T(8,128)} %pad_maximum_fusion.1) | data formatting | bytes 4915200 | tf_op jit(solution)/shard_map/reshape | solution.py:30
  63.2 1.9 %multiply_reduce_fusion = f32[12,25,256]{2,1,0:T(8,128)} fusion(f32[12,8,25,256]{3,2,1,0:T(8,128)S(1)} %reshape.351, f32[8,256]{1,0:T(8,128)} %tile.9), kind=kLoop, calls=%fused_computation.12 | loop fusion | flops 1152000 | bytes 2772992 | tf_op jit(solution)/shard_map/reduce_sum | solution.py:34
  65.3 2.0 %fusion.51 = f32[12,25,32]{1,2,0:T(8,128)S(1)} fusion(f32[12,25,256]{2,1,0:T(8,128)} %multiply_reduce_fusion, f32[256,32,1]{0,1,2:T(8,128)S(1)} %reshape.365), kind=kOutput, calls=%fused_computation.136 | convolution fusion | flops 29491200 | bytes 378368 | tf_op jit(solution)/shard_map/lpC,CD->lpD/dot_general | solution.py:92
  67.3 1.5 convolution_bitcast_fusion.6
  68.8 1.5 convolution_bitcast_fusion.5
  70.4 0.5 reshape.352
  71.0 0.5 multiply_reduce_fusion.3
  71.8 0.7 copy.208
  72.8 0.7 copy.207
  73.8 0.6 convolution_bitcast_fusion.10
  74.4 0.6 convolution_bitcast_fusion.11
  75.3 0.5 convolution_bitcast_fusion.4
  75.8 0.5 fusion.15
  76.4 0.5 reshape.357
  76.9 0.5 multiply_reduce_fusion.2
  77.7 13.9 %psum.7 = f32[12,25,16]{1,2,0:T(8,128)S(1)} all-reduce(f32[12,25,16]{1,2,0:T(8,128)S(1)} %reduce_sum.49), channel_id=1, replica_groups=mesh['groups'=2,'leaf'=4,'state'=2,'sub'=2] {'state','sub'}, use_global_device_ids=true, to_apply=%region_5.6 | all-reduce | flops 4800 | bytes 38400 | tf_op jit(solution)/shard_map/psum | solution.py:197
  91.6 1.4 fusion.50
  93.0 0.4 convolution_bitcast_fusion.14
  93.4 0.4 convolution_bitcast_fusion.15
  95.9 0.4 convolution_bitcast_fusion.13
  97.5 0.6 dynamic_slice.3
  98.0 0.7 fusion.38
  98.9 1.0 copy.210
  99.9 0.8 copy.195
  100.7 0.6 dynamic-slice
  101.3 20.8 %reduce-scatter.4.cloned.1.call-done = f32[64,512]{1,0:T(8,128)} async-done(((f32[256,512]{1,0:T(8,128)}), f32[64,512]{1,0:T(8,128)}) %reduce-scatter.4.cloned.1.call-update) | async-done | bytes 131088
  122.0 1.0 copy.211
  124.5 10.3 %all-reduce = bf16[4,4,1024]{2,1,0:T(4,128)(2,1)S(1)} all-reduce(bf16[4,4,1024]{2,1,0:T(4,128)(2,1)S(1)} %copy.209), channel_id=3, replica_groups=mesh['groups'=2,'leaf'=4,'state'=2,'sub'=2] {'state','sub'}, use_global_device_ids=true, to_apply=%region_7.8.clone | all-reduce | flops 16384 | bytes 65536
  134.7 0.7 constant_dynamic-slice_fusion
  135.4 0.5 broadcast.208
  135.9 0.7 reduce.2
  136.6 0.6 reshape.377
  137.3 3.5 %all-to-all-start = ((bf16[4,2,512]{2,1,0:T(2,128)(2,1)}), bf16[4,2,512]{2,1,0:T(2,128)(2,1)S(1)}, u32[]{:S(2)}, u32[]{:S(2)}) async-start(bf16[4,2,512]{2,1,0:T(2,128)(2,1)} %reshape.377), calls=%async_computation | async-start | bytes 16384 | tf_op jit(solution)/shard_map/all_to_all | solution.py:223
  140.7 5.3 %all-to-all-done = bf16[4,2,512]{2,1,0:T(2,128)(2,1)S(1)} async-done(((bf16[4,2,512]{2,1,0:T(2,128)(2,1)}), bf16[4,2,512]{2,1,0:T(2,128)(2,1)S(1)}, u32[]{:S(2)}, u32[]{:S(2)}) %all-to-all-start) | async-done | bytes 8224 | tf_op jit(solution)/shard_map/all_to_all | solution.py:223
  146.3 15.7 %convolution_bitcast_fusion = f32[2,2,4,1,4096]{4,2,1,0,3:T(4,128)S(1)} fusion(bf16[2,2,4,256]{3,2,1,0:T(4,128)(2,1)S(1)} %dot_general.132, f32[4096]{0:T(1024)S(1)} %fusion.28, s32[4096]{0:T(1024)S(1)} %add_select_fusion.2, s32[256]{0:T(256)S(1)} %iota_add_fusion), kind=kOutput, calls=%fused_computation.5 | convolution fusion | flops 50331648 | bytes 304128 | tf_op jit(solution)/shard_map/dot_general | solution.py:162
  162.1 0.8 copy.202
  (113 shorter events, 10.7 us)
Async XLA Ops:
  6.5 90.2 %copy-start = (bf16[1,32,25,256]{3,1,2,0:T(8,128)(2,1)S(1)}, bf16[1,32,25,256]{3,1,2,0:T(8,128)(2,1)}, u32[]{:S(2)}) copy-start(bf16[1,32,25,256]{3,1,2,0:T(8,128)(2,1)} %param.26) | copy-start | bytes 1228804
  6.5 115.5 %reduce-scatter.4.cloned.1.call-start = ((), (), s32[]{:S(2)}) async-start(), calls=%async_computation.2 | async-start | bytes 655360
  11.7 5.5 %copy-start.12 = (s32[64]{0:T(128)S(1)}, s32[64]{0:T(128)}, u32[]{:S(2)}) copy-start(s32[64]{0:T(128)} %param.16) | copy-start | bytes 772
  22.7 5.5 %copy-start.3 = (f32[12,200,25]{1,2,0:T(8,128)}, f32[12,200,25]{1,2,0:T(8,128)S(1)}, u32[]{:S(2)}) copy-start(f32[12,200,25]{1,2,0:T(8,128)S(1)} %squeeze.60) | copy-start | bytes 720004
  37.2 2.1 %copy-start.8 = (f32[2,25,2,12,2,12]{1,4,5,3,2,0:T(2,128)S(1)}, f32[2,25,2,12,2,12]{1,4,5,3,2,0:T(2,128)}, u32[]{:S(2)}) copy-start(f32[2,25,2,12,2,12]{1,4,5,3,2,0:T(2,128)} %param.21) | copy-start | bytes 345604
  43.3 5.1 %copy-start.1 = (f32[8,2,12,25,25]{4,1,3,2,0:T(2,128)S(1)}, f32[8,2,12,25,25]{4,1,3,2,0:T(2,128)}, u32[]{:S(2)}) copy-start(f32[8,2,12,25,25]{4,1,3,2,0:T(2,128)} %param.20) | copy-start | bytes 1440004
  51.4 1.3 copy-start.2
  53.1 5.5 %copy-start.5 = (f32[12,200,25]{1,2,0:T(8,128)}, f32[12,200,25]{1,2,0:T(8,128)S(1)}, u32[]{:S(2)}) copy-start(f32[12,200,25]{1,2,0:T(8,128)S(1)} %squeeze.65) | copy-start | bytes 720004
  63.2 1.9 %copy-start.13 = (s32[16]{0:T(128)S(1)}, s32[16]{0:T(128)}, u32[]{:S(2)}) copy-start(s32[16]{0:T(128)} %param.17) | copy-start | bytes 196
  63.2 1.9 %copy-start.11 = (f32[16,16]{0,1:T(8,128)S(1)}, f32[16,16]{0,1:T(8,128)}, u32[]{:S(2)}) copy-start(f32[16,16]{0,1:T(8,128)} %fusion.33) | copy-start | bytes 3076
  68.8 2.1 %copy-start.14 = (s32[2]{0:T(128)S(1)}, s32[2]{0:T(128)}, u32[]{:S(2)}) copy-start(s32[2]{0:T(128)} %param.19) | copy-start | bytes 28
  70.4 1.4 copy-start.9
  72.8 2.5 %copy-start.4 = (f32[12,200,25]{1,2,0:T(8,128)S(1)}, f32[12,200,25]{1,2,0:T(8,128)}, u32[]{:S(2)}) copy-start(f32[12,200,25]{1,2,0:T(8,128)} %squeeze.64) | copy-start | bytes 720004
  73.5 2.3 %copy-start.6 = (f32[12,200,25]{1,2,0:T(8,128)S(1)}, f32[12,200,25]{1,2,0:T(8,128)}, u32[]{:S(2)}) copy-start(f32[12,200,25]{1,2,0:T(8,128)} %copy-done.5) | copy-start | bytes 720004
  76.9 17.2 %copy-start.7 = (f32[1,2,25,2,32,2,12]{4,5,6,3,2,1,0:T(2,128)S(1)}, f32[1,2,25,2,32,2,12]{4,5,6,3,2,1,0:T(2,128)}, u32[]{:S(2)}) copy-start(f32[1,2,25,2,32,2,12]{4,5,6,3,2,1,0:T(2,128)} %param.24) | copy-start | bytes 921604
  95.2 2.3 %copy-start.15 = (f32[4]{0:T(128)S(1)}, f32[4]{0:T(128)}, u32[]{:S(2)}) copy-start(f32[4]{0:T(128)} %param.25) | copy-start | bytes 52
  97.1 2.8 %copy-start.10 = (bf16[64,32,32]{0,2,1:T(8,128)(2,1)S(1)}, bf16[64,32,32]{0,2,1:T(8,128)(2,1)}, u32[]{:S(2)}) copy-start(bf16[64,32,32]{0,2,1:T(8,128)(2,1)} %param.27) | copy-start | bytes 393220
  97.4 3.3 %copy-start.16 = (u32[32]{0:T(128)S(1)}, u32[32]{0:T(128)}, u32[]{:S(2)}) copy-start(u32[32]{0:T(128)} %constant.84) | copy-start | bytes 388
  137.3 8.8 %all-to-all-start = ((bf16[4,2,512]{2,1,0:T(2,128)(2,1)}), bf16[4,2,512]{2,1,0:T(2,128)(2,1)S(1)}, u32[]{:S(2)}, u32[]{:S(2)}) async-start(bf16[4,2,512]{2,1,0:T(2,128)(2,1)} %reshape.377), calls=%async_computation | async-start | bytes 16384 | tf_op jit(solution)/shard_map/all_to_all | solution.py:223
Sparse Core Ops, SparseCore 0:
  100.0 22.0 reduce-scatter.3
where the time goes:
time: 173 us; the launch traced here: 170 us
  local copies, waits for them, and re-layouts  50.4 us (29%)
  matrix products  37.5 us (22%)
  waiting for transfers between devices  26.1 us (15%)
  blocking collectives  24.2 us (14%)
  between operations  15.3 us (9%)
  other arithmetic  13 us (8%)
  starting transfers between devices  3.46 us (2%)
    unnamed x2, waiting for transfers between devices  20.8 us
    dot_general x1, matrix products, synthesize(): product = jnp.dot(spectrum, table, preferred_element_type=jnp.float32)  15.7 us
    psum x1, blocking collectives, on_device(): owner_sum = lax.psum(partial_owner, ('state', 'sub'))  13.9 us
    unnamed x1, blocking collectives  10.3 us
    slice x4, local copies, waits for them, and re-layouts, turn_select(): mats[0]  8.68 us
    dot_general x4, matrix products, turn_select(): jnp.einsum('lQp,lpC->lQC', mats[1], vectors, precision=lax.Precision.HIGH...  7.41 us
    dot_general x4, matrix products, turn_select(): jnp.einsum('lQp,lpC->lQC', mats[0], vectors, precision=lax.Precision.HIGH...  7.38 us
    reshape x4, local copies, waits for them, and re-layouts, turn_select(): complex_join(first, second, width // 2).reshape(degrees, 8, orders, width)  6.15 us
  transfers between devices with their start and end apart: 2, of which 2 were waited for; matrix products, arithmetic and copies ran while one was open for 1% of the time, Pallas kernels for 0%

commit v1 on v0

v1 whole, which is shorter than its diff:
```python
import functools
import math

import jax
import jax.numpy as jnp
from jax import lax
from jax.experimental import pallas as pl
from jax.experimental.pallas import tpu as pltpu
from jax.sharding import PartitionSpec as P

SBLK = 4
PHI = 2048
LP = 16
QP = 32
MESH = pl.DeviceIdType.MESH


def lane_ids():
    lane = lax.broadcasted_iota(jnp.int32, (1, 128), 1)
    return lane, (lane % 64) // 4


def spread_matrix():
    row = lax.broadcasted_iota(jnp.int32, (128, 128), 0)
    col = lax.broadcasted_iota(jnp.int32, (128, 128), 1)
    same = (row // 64 == col // 64) & (row % 4 == col % 4)
    return jnp.where(same, 1.0, 0.0).astype(jnp.bfloat16)


def dot(a, b):
    return jnp.dot(a, b, preferred_element_type=jnp.float32)


def axial_operand(y_ref, q):
    pieces = [y_ref[pl.ds(part * QP + q, LP, stride=2 * QP), :] for part in range(2)]
    here = jnp.concatenate(pieces, axis=0)
    there = pltpu.roll(here, 64, 1)
    return jnp.concatenate([here, there], axis=0).astype(jnp.bfloat16)


def axial_pass(y_ref, z_ref, a_ref, orders):
    lane, _ = lane_ids()
    low = lane < 64
    for q in range(orders):
        r = dot(a_ref[q], axial_operand(y_ref, q))
        z = jnp.where(low, r[: 2 * LP], r[2 * LP :])
        for part in range(2):
            z_ref[pl.ds(part * QP + q, LP, stride=2 * QP), :] = z[part * LP : (part + 1) * LP]


def local_kernel(box_ref, xs_ref, code_ref, f_ref, a1_ref, a2_ref, out_ref, v_ref, y_ref, z_ref):
    degrees = f_ref.shape[0]
    orders = a1_ref.shape[0]
    lane, rep = lane_ids()
    width = 2 * QP
    y_ref[...] = jnp.zeros_like(y_ref)
    z_ref[...] = jnp.zeros_like(z_ref)
    slots = xs_ref.shape[1] // 8
    row = lax.broadcasted_iota(jnp.int32, (8 * slots, 128), 0) // slots
    col = lax.broadcasted_iota(jnp.int32, (8 * slots, 128), 1)
    keep = (
        (row // 4 == col // 64) & (row % 4 == col % 4) & ((col % 64) // 4 == code_ref[...])
    )
    spread = jnp.where(keep, 1.0, 0.0).astype(jnp.bfloat16)
    v_ref[...] = dot(xs_ref[...], spread).astype(jnp.bfloat16)
    octant = rep // 2
    box = rep % 2

    for level in range(2):
        for l in range(degrees):
            v = v_ref[l * width : (l + 1) * width, :]
            if level == 0:
                r = dot(f_ref[l].reshape(8 * width, width), v)
                acc = r[:width]
                for o in range(1, 8):
                    acc = jnp.where(octant == o, r[o * width : (o + 1) * width], acc)
            else:
                acc = dot(f_ref[l, box_ref[0]], v)
                acc = jnp.where(box == 1, dot(f_ref[l, box_ref[1]], v), acc)
            y_ref[l * width : (l + 1) * width, :] = acc
        axial_pass(y_ref, z_ref, a1_ref if level == 0 else a2_ref, orders)
        for l in range(degrees):
            z = z_ref[l * width : (l + 1) * width, :]
            if level == 0:
                mats = f_ref[l].reshape(8 * width, width)
                parts = [jnp.where(octant == o, z, 0.0) for o in range(8)]
            else:
                mats = jnp.concatenate([f_ref[l, box_ref[0]], f_ref[l, box_ref[1]]], axis=0)
                parts = [jnp.where(box == b, z, 0.0) for b in range(2)]
            stacked = jnp.concatenate(parts, axis=0).astype(jnp.bfloat16)
            r = lax.dot_general(
                mats, stacked, (((0,), (0,)), ((), ())), preferred_element_type=jnp.float32
            )
            if level == 0:
                v_ref[l * width : (l + 1) * width, :] = r.astype(jnp.bfloat16)
            else:
                y_ref[l * width : (l + 1) * width, :] = r
    total = degrees * width
    m = y_ref[:total, :]
    hi = m.astype(jnp.bfloat16)
    lo = (m - hi.astype(jnp.float32)).astype(jnp.bfloat16)
    mix = spread_matrix()
    full = dot(hi, mix) + dot(lo, mix)
    rows = total // 16
    packed = full[:rows]
    for r in range(1, 16):
        packed = jnp.where(rep == r, full[r * rows : (r + 1) * rows], packed)
    out_ref[...] = packed


def make_tables(tab_c, tab_s):
    orders = tab_c.shape[0]
    j = lax.broadcasted_iota(jnp.int32, (16, 128), 0) - orders // 2
    k = lax.broadcasted_iota(jnp.int32, (16, 128), 1)
    step = 2.0 * math.pi / PHI
    turns = []
    for a in range(PHI // 128):
        angle = (jnp.bitwise_and(j * (128 * a), PHI - 1)).astype(jnp.float32) * step
        turns.append((jnp.cos(angle), jnp.sin(angle)))

    def body(i, carry):
        r0 = pl.multiple_of(i * 16, 16)
        angle = (jnp.bitwise_and((j + r0) * k, PHI - 1)).astype(jnp.float32) * step
        c1 = jnp.cos(angle)
        s1 = jnp.sin(angle)
        for a, (c2, s2) in enumerate(turns):
            cols = slice(a * 128, (a + 1) * 128)
            tab_c[pl.ds(r0, 16), cols] = (c1 * c2 - s1 * s2).astype(jnp.bfloat16)
            tab_s[pl.ds(r0, 16), cols] = (s1 * c2 + c1 * s2).astype(jnp.bfloat16)
        return carry

    lax.fori_loop(0, orders // 16, body, 0)


def owner_kernel(
    dims,
    packed_ref,
    fo_ref,
    ao_ref,
    cos_ref,
    sin_ref,
    turn_ref,
    ang_ref,
    out_ref,
    recv1,
    y_ref,
    zq_ref,
    vals_ref,
    sbuf,
    recv2,
    root_ref,
    fbuf,
    recv3,
    tab_c,
    tab_s,
    send1,
    rsem1,
    send2,
    rsem2,
    send3,
    rsem3,
):
    leaf_size, state_size, sub_size = dims
    group = state_size * sub_size
    holders = leaf_size * group
    my_groups = lax.axis_index("groups")
    my_leaf = lax.axis_index("leaf")
    my_state = lax.axis_index("state")
    my_sub = lax.axis_index("sub")
    my_g = my_state * sub_size + my_sub
    me = my_leaf * group + my_g
    degrees = fo_ref.shape[0]
    q_orders = ao_ref.shape[0]
    nloc = turn_ref.shape[0]
    orders = turn_ref.shape[2]
    width = 2 * QP
    lane, rep = lane_ids()
    low = lane < 64

    def device(index):
        g = lax.rem(index, group)
        return (my_groups, index // group, g // sub_size, lax.rem(g, sub_size))

    barrier = pltpu.get_barrier_semaphore()

    def greet(d, carry):
        pl.semaphore_signal(
            barrier, inc=1, device_id=device(lax.rem(me + d, holders)), device_id_type=MESH
        )
        return carry

    lax.fori_loop(1, holders, greet, 0)
    pl.semaphore_wait(barrier, holders - 1)

    copies = []
    for d in range(1, group):
        target = my_leaf * group + lax.rem(my_g + d, group)
        copy = pltpu.make_async_remote_copy(
            src_ref=packed_ref,
            dst_ref=recv1.at[d - 1],
            send_sem=send1.at[d - 1],
            recv_sem=rsem1.at[d - 1],
            device_id=device(target),
            device_id_type=MESH,
        )
        copy.start()
        copies.append(copy)

    y_ref[...] = jnp.zeros_like(y_ref)
    zq_ref[...] = jnp.zeros_like(zq_ref)
    make_tables(tab_c, tab_s)

    for copy in copies:
        copy.wait()
    packed = packed_ref[...]
    for d in range(1, group):
        packed = packed + recv1[d - 1]
    parts = [jnp.where(rep == r, packed, 0.0) for r in range(16)]
    vectors = dot(
        jnp.concatenate(parts, axis=0).astype(jnp.bfloat16), spread_matrix()
    ).astype(jnp.bfloat16)
    for l in range(degrees):
        y_ref[l * width : (l + 1) * width, :] = dot(
            fo_ref[l], vectors[l * width : (l + 1) * width]
        )
    for q in range(q_orders):
        r = dot(ao_ref[q], axial_operand(y_ref, q))
        zq_ref[q * 2 * nloc : (q + 1) * 2 * nloc, :] = jnp.where(
            low, r[: 2 * nloc], r[2 * nloc :]
        )

    cosine = cos_ref[...]
    sine = sin_ref[...]
    for block in range(nloc // 8):
        gathered = jnp.zeros((QP, 128), jnp.float32)
        for n8 in range(8):
            n = block * 8 + n8
            real = zq_ref[pl.ds(n, QP, stride=2 * nloc), :]
            imag = zq_ref[pl.ds(nloc + n, QP, stride=2 * nloc), :]
            both = jnp.where(rep % 2 == 0, real, imag)
            gathered = jnp.where(rep // 2 == n8, both, gathered)
        flipped = gathered.T
        for n8 in range(8):
            n = block * 8 + n8
            framed = jnp.concatenate(
                [flipped[n8 * 8 : n8 * 8 + 8], flipped[64 + n8 * 8 : 72 + n8 * 8]], axis=0
            ).astype(jnp.bfloat16)
            values = dot(framed, turn_ref[n])
            for u in range(2):
                v = values[u * 8 : u * 8 + 8]
                vals_ref[n, u * 8 : u * 8 + 8, :] = cosine * v + sine * pltpu.roll(v, 4, 0)

    half = nloc // 2
    for m in range(orders // 128):
        cols = slice(m * 128, (m + 1) * 128)
        for n in range(half):
            a = vals_ref[n, :, cols]
            b = vals_ref[n + half, :, cols]
            rows = slice(n * 16, (n + 1) * 16)
            sbuf[2 * m, rows, :] = jnp.where(low, a, pltpu.roll(b, 64, 1)).astype(jnp.bfloat16)
            sbuf[2 * m + 1, rows, :] = jnp.where(low, pltpu.roll(a, 64, 1), b).astype(
                jnp.bfloat16
            )

    copies = []
    for d in range(1, leaf_size):
        to_leaf = lax.rem(my_leaf + d, leaf_size)
        copy = pltpu.make_async_remote_copy(
            src_ref=sbuf.at[to_leaf],
            dst_ref=recv2.at[d - 1],
            send_sem=send2.at[d - 1],
            recv_sem=rsem2.at[d - 1],
            device_id=device(to_leaf * group + my_g),
            device_id_type=MESH,
        )
        copy.start()
        copies.append(copy)
    for copy in copies:
        copy.wait()
    root = sbuf[my_leaf].astype(jnp.float32)
    for d in range(1, leaf_size):
        root = root + recv2[d - 1].astype(jnp.float32)
    root_ref[...] = root.astype(jnp.bfloat16).astype(jnp.float32)

    lats = ang_ref.shape[1] // 2
    sign = jnp.where(lax.broadcasted_iota(jnp.int32, (8, 128), 0) < 4, -1.0, 1.0)

    def latitude(h, carry):
        theta = jnp.zeros((8, 128), jnp.float32)
        cross = jnp.zeros((8, 128), jnp.float32)
        for n in range(half):
            a0 = ang_ref[n, pl.ds(h, 1), :]
            a1 = ang_ref[n, pl.ds(lats + h, 1), :]
            r0 = root_ref[n * 16 : n * 16 + 8, :]
            r1 = root_ref[n * 16 + 8 : n * 16 + 16, :]
            theta = theta + (a0 * r0 + a1 * r1)
            cross = cross + (a1 * r0 + a0 * r1)
        theta = theta + pltpu.roll(theta, 64, 1)
        cross = cross + pltpu.roll(cross, 64, 1)
        phi = sign * pltpu.roll(cross, 4, 0)
        fbuf[h] = jnp.concatenate([theta, phi], axis=0).astype(jnp.bfloat16)
        return carry

    lax.fori_loop(0, lats, latitude, 0)

    def field_copy(d):
        target = lax.rem(me + d, holders)
        return pltpu.make_async_remote_copy(
            src_ref=fbuf.at[target],
            dst_ref=recv3.at[me],
            send_sem=send3.at[d - 1],
            recv_sem=rsem3.at[d - 1],
            device_id=device(target),
            device_id_type=MESH,
        )

    def start(d, carry):
        field_copy(d).start()
        return carry

    def finish(d, carry):
        field_copy(d).wait_send()
        source = lax.rem(me + holders - d, holders)
        pltpu.make_async_remote_copy(
            src_ref=fbuf.at[source],
            dst_ref=recv3.at[source],
            send_sem=send3.at[d - 1],
            recv_sem=rsem3.at[d - 1],
            device_id=device(source),
            device_id_type=MESH,
        ).wait_recv()
        return carry

    lax.fori_loop(1, holders, start, 0)
    recv3[me] = fbuf[me]
    lax.fori_loop(1, holders, finish, 0)

    pieces = []
    for leaf in range(leaf_size):
        total = recv3[leaf * group].astype(jnp.float32)
        for g in range(1, group):
            total = total + recv3[leaf * group + g].astype(jnp.float32)
        pieces.append(total)
    spectrum = jnp.concatenate(
        [
            jnp.where(low, pieces[2 * m], pieces[2 * m + 1]).astype(jnp.bfloat16)
            for m in range(leaf_size // 2)
        ],
        axis=1,
    )
    scale = 1.0 / math.sqrt(orders)
    for tile in range(PHI // 512):
        cols = slice(tile * 512, (tile + 1) * 512)
        first = dot(spectrum, tab_c[:, cols])
        second = dot(spectrum, tab_s[:, cols])
        for c in range(2):
            rows = slice(c * 8, c * 8 + 8)
            turned = pltpu.roll(second[rows], 4, 0)
            out_ref[rows, cols] = (first[rows] + jnp.tile(sign, (1, 4)) * turned) * scale


def pad_last(x, *sizes):
    skip = x.ndim - len(sizes)
    return jnp.pad(
        x, [(0, 0)] * skip + [(0, s - n) for s, n in zip(sizes, x.shape[skip:], strict=True)]
    )


def rotation_blocks(real, imag):
    real = pad_last(real.astype(jnp.bfloat16), QP, QP)
    imag = pad_last(imag.astype(jnp.bfloat16), QP, QP)
    return jnp.concatenate(
        [jnp.concatenate([real, -imag], -1), jnp.concatenate([imag, real], -1)], -2
    )


def axial_blocks(axial, out_rows):
    mats = axial.astype(jnp.bfloat16)
    mats = jnp.stack([mats[:, :, 0], mats[:, :, 1, :, ::-1]], axis=2)
    mats = jnp.transpose(mats, (0, 1, 2, 4, 3, 5))
    mats = pad_last(mats, out_rows, LP)
    real, imag = mats[0], mats[1]
    blocks = jnp.stack([jnp.stack([real, -imag], 0), jnp.stack([imag, real], 0)], 0)
    blocks = jnp.transpose(blocks, (2, 3, 0, 5, 4, 1, 6))
    orders = axial.shape[1]
    return blocks.reshape(orders, 4 * out_rows, 4 * LP)


def on_device(
    dims,
    sphere_coef,
    live_blocks,
    cluster,
    leaf_parent,
    leaf_octant,
    box_octant,
    rotation,
    axial_one,
    axial_two,
    owner_rotation,
    owner_axial,
    owner_angle,
    turn_table,
    angular_table,
):
    leaf_size, state_size, sub_size = dims
    group = state_size * sub_size
    holders = leaf_size * group
    degrees, morders = sphere_coef.shape[:2]
    slots = sphere_coef.shape[-1]
    bf16 = jnp.bfloat16
    f32 = jnp.float32

    leaf_code = leaf_octant * 2 + leaf_parent
    member = cluster[:, None] == jnp.arange(leaf_code.shape[0], dtype=jnp.int32)[None, :]
    code = jnp.sum(jnp.where(member, leaf_code[None, :], 0), axis=1)
    alive = jnp.arange(slots, dtype=jnp.int32) // (slots // SBLK) < live_blocks[0]
    code = jnp.where(alive, code, -1)
    code = jnp.broadcast_to(code[None, :], (8, slots)).reshape(8 * slots, 1)

    xs = jnp.transpose(sphere_coef, (0, 2, 1, 3, 4, 5)).reshape(degrees, 2, morders, 8 * slots)
    xs = pad_last(xs, QP, 8 * slots).reshape(degrees * 2 * QP, 8 * slots)
    turns = jnp.transpose(rotation, (1, 2, 0, 3, 4))
    f = rotation_blocks(turns[0], turns[1])
    a1 = axial_blocks(axial_one, LP)
    a2 = axial_blocks(axial_two, LP)
    rows = degrees * 2 * QP
    vmem = pl.BlockSpec(memory_space=pltpu.VMEM)
    packed = pl.pallas_call(
        local_kernel,
        out_shape=jax.ShapeDtypeStruct((rows // 16, 128), f32),
        in_specs=[pl.BlockSpec(memory_space=pltpu.SMEM)] + [vmem] * 5,
        out_specs=vmem,
        scratch_shapes=[
            pltpu.VMEM((rows, 128), bf16),
            pltpu.VMEM((LP * 2 * QP, 128), f32),
            pltpu.VMEM((LP * 2 * QP, 128), f32),
        ],
        compiler_params=pltpu.CompilerParams(vmem_limit_bytes=32 * 1024 * 1024),
    )(box_octant, xs, code, f, a1, a2)

    fo = rotation_blocks(owner_rotation[0, 0], owner_rotation[0, 1])
    nloc = turn_table.shape[1]
    orders = turn_table.shape[3]
    ao = axial_blocks(owner_axial[0], nloc)
    azimuth = owner_angle[lax.axis_index("leaf")]
    order_values = (jnp.arange(orders, dtype=jnp.int32) - orders // 2).astype(f32)
    flip = jnp.where(jnp.arange(8) < 4, 1.0, -1.0).astype(f32)
    cosine = jnp.broadcast_to(jnp.cos(order_values * azimuth)[None, :], (8, orders))
    sine = flip[:, None] * jnp.sin(order_values * azimuth)[None, :]
    turn = pad_last(turn_table[0], QP, orders)
    own = angular_table.shape[0]
    ang = jnp.transpose(angular_table, (1, 2, 0)).reshape(2, nloc // 2, -1, own)
    ang = jnp.concatenate([ang[0], ang[1]], axis=-1).astype(f32)
    lats = ang.shape[1] // 2
    assert own == 64 and lats == holders and orders == 64 * leaf_size

    out = pl.pallas_call(
        functools.partial(owner_kernel, dims),
        out_shape=jax.ShapeDtypeStruct((16, PHI), f32),
        in_specs=[vmem] * 7,
        out_specs=vmem,
        scratch_shapes=[
            pltpu.VMEM((group - 1, rows // 16, 128), f32),
            pltpu.VMEM((LP * 2 * QP, 128), f32),
            pltpu.VMEM((QP * 2 * nloc, 128), f32),
            pltpu.VMEM((nloc, 16, orders), f32),
            pltpu.VMEM((leaf_size, 8 * nloc, 128), bf16),
            pltpu.VMEM((leaf_size - 1, 8 * nloc, 128), bf16),
            pltpu.VMEM((8 * nloc, 128), f32),
            pltpu.VMEM((lats, 16, 128), bf16),
            pltpu.VMEM((holders, 16, 128), bf16),
            pltpu.VMEM((orders, PHI), bf16),
            pltpu.VMEM((orders, PHI), bf16),
            pltpu.SemaphoreType.DMA((group - 1,)),
            pltpu.SemaphoreType.DMA((group - 1,)),
            pltpu.SemaphoreType.DMA((leaf_size - 1,)),
            pltpu.SemaphoreType.DMA((leaf_size - 1,)),
            pltpu.SemaphoreType.DMA((holders - 1,)),
            pltpu.SemaphoreType.DMA((holders - 1,)),
        ],
        compiler_params=pltpu.CompilerParams(
            collective_id=0, has_side_effects=True, vmem_limit_bytes=48 * 1024 * 1024
        ),
    )(packed, fo, ao, cosine, sine, turn, ang)
    out = out.reshape(2, 2, 4, PHI)
    return jnp.transpose(out, (2, 0, 1, 3))[None]


def solution(mesh):
    dims = (mesh.shape["leaf"], mesh.shape["state"], mesh.shape["sub"])
    split = ("groups", "leaf", "state", "sub")
    return jax.shard_map(
        functools.partial(on_device, dims),
        mesh=mesh,
        in_specs=(
            P(None, None, None, None, None, split),
            P(split),
            P(split),
            P(split),
            P(split),
            P(split),
            P(),
            P(),
            P(),
            P(("groups", "leaf"), None, None, None, None),
            P(("groups", "leaf"), None, None, None, ("state", "sub"), None, None),
            P("groups"),
            P(("groups", "leaf"), ("state", "sub"), None, None),
            P("leaf", ("state", "sub"), None),
        ),
        out_specs=P(split, None, None, None, None),
        check_vma=False,
    )
```

time: 173 us -> 68.5 us (0.40); the launches traced: 170 us -> 68.2 us
  matrix products: 37.5 us -> 0 us
  local copies, waits for them, and re-layouts: 50.4 us -> 18.5 us
  Pallas kernels: 0 us -> 28.7 us
  waiting for transfers between devices: 26.1 us -> 0 us
  blocking collectives: 24.2 us -> 0 us
  between operations: 15.3 us -> 1.14 us
  other arithmetic: 13 us -> 20 us
  starting transfers between devices: 3.46 us -> 0 us
    dot_general x21 -> x0, matrix products: 37.5 us -> none  [the longest x1 15.7 us: synthesize(): product = jnp.dot(spectrum, table, preferred_element_type=jnp.float32)]
    pallas_call x0 -> x2, Pallas kernels: none -> 28.7 us  [the longest x1 24.7 us: on_device(): pl.pallas_call(functools.partial(owner_kernel, dims), out_shape=jax.Shape...]
    unnamed x2 -> x0, waiting for transfers between devices: 20.8 us -> none
    psum x1 -> x0, blocking collectives: 13.9 us -> none  [on_device(): owner_sum = lax.psum(partial_owner, ('state', 'sub'))]
    slice x13 -> x4, local copies, waits for them, and re-layouts: 13.4 us -> 0.85 us  [the longest x3 0.83 us: axial_blocks(): mats = jnp.stack([mats[:, :, 0], mats[:, :, 1, :, ::-1]], axis=2)]
    unnamed x1 -> x0, blocking collectives: 10.3 us -> none
    squeeze x14 -> x0, local copies, waits for them, and re-layouts: 9.46 us -> none  [the longest x2 2.81 us: turn_select(): mats[1]]
    transpose x0 -> x6, other arithmetic: none -> 8.2 us  [the longest x3 6.24 us: axial_blocks(): blocks = jnp.transpose(blocks, (2, 3, 0, 5, 4, 1, 6))]
  transfers between devices with their start and end apart: 2 -> 0, of which waited for: 2 -> 0; matrix products, arithmetic and copies ran while one was open for 1% -> 0% of each run, Pallas kernels for 0% -> 0%
where the time goes in v1:
time: 68.5 us; the launch traced here: 68.2 us
  Pallas kernels  28.7 us (42%)
  other arithmetic  20 us (29%)
  local copies, waits for them, and re-layouts  18.5 us (27%)
  between operations  1.14 us (2%)
    pallas_call x1, Pallas kernels, on_device(): pl.pallas_call(functools.partial(owner_kernel, dims), out_shape=jax.Shape...  24.7 us
    transpose x3, other arithmetic, axial_blocks(): blocks = jnp.transpose(blocks, (2, 3, 0, 5, 4, 1, 6))  6.24 us
    another operation x3, other arithmetic, axial_blocks(): jnp.stack([jnp.stack([real, -imag], 0), jnp.stack([imag, real], 0)], 0)  5.28 us
    pallas_call x1, Pallas kernels, on_device(): pl.pallas_call(local_kernel, out_shape=jax.ShapeDtypeStruct((rows // 16,...  3.94 us
    rev x3, local copies, waits for them, and re-layouts, axial_blocks(): mats = jnp.stack([mats[:, :, 0], mats[:, :, 1, :, ::-1]], axis=2)  3.59 us
    reshape x2, local copies, waits for them, and re-layouts, on_device(): jnp.transpose(sphere_coef, (0, 2, 1, 3, 4, 5))  3.36 us
    reshape x4, local copies, waits for them, and re-layouts, axial_blocks(): return blocks.reshape(orders, 4 * out_rows, 4 * LP)  2.94 us
    unnamed x23, local copies, waits for them, and re-layouts  2.9 us

profile of v1, /device:TPU:0, one launch (start us, length us, event | category | flops | bytes accessed | tf_op | source)
XLA Modules:
  0.0 68.2 jit_solution(547539261788126886)
XLA Ops:
  0.0 1.3 %convert_element_type.59 = bf16[2,25,2,12,2,12]{1,4,5,3,2,0:T(2,128)(2,1)S(1)} convert(f32[2,25,2,12,2,12]{1,4,5,3,2,0:T(2,128)} %param.22) | non-fusion elementwise | flops 28800 | bytes 172800 | tf_op jit(solution)/shard_map/convert_element_type | solution.py:378
  1.3 0.2 fusion.6
  1.5 1.0 %rev.10 = bf16[2,25,1,12,2,12]{1,4,5,3,2,0:T(2,128)(2,1)S(1)} reverse(bf16[2,25,1,12,2,12]{1,4,5,3,2,0:T(2,128)(2,1)S(1)} %get-tuple-element.22), dimensions={4} | reverse | bytes 57600 | tf_op jit(solution)/shard_map/rev | solution.py:379
  2.4 0.5 maximum_bitcast_fusion.11
  2.9 0.6 fusion.3
  3.5 1.4 %maximum_bitcast_fusion.8 = (bf16[1,2,25,2,2,16,16]{2,4,6,5,3,1,0:T(2,128)(2,1)S(1)}, bf16[1,2,25,2,2,16,16]{2,4,6,5,3,1,0:T(2,128)(2,1)S(1)}) fusion(bf16[1,25,2,2,16,16]{1,3,5,4,2,0:T(2,128)(2,1)S(1)} %get-tuple-element.7, bf16[1,25,2,2,16,16]{1,3,5,4,2,0:T(2,128)(2,1)S(1)} %get-tuple-element.20, bf16[1,25,2,2,16,16]{1,3,5,4,2,0:T(2,128)(2,1)S(1)} %get-tuple-element.8), kind=kLoop, calls=%fused_computation.16 | loop fusion | flops 102400 | bytes 358400 | tf_op jit(solution)/shard_map/stack | solution.py:383
  5.0 1.8 %maximum_bitcast_fusion.2 = bf16[25,2,2,16,2,2,16]{0,4,6,3,1,5,2:T(2,128)(2,1)S(1)} fusion(bf16[1,2,25,2,2,16,16]{2,4,6,5,3,1,0:T(2,128)(2,1)S(1)} %get-tuple-element.29, bf16[1,2,25,2,2,16,16]{2,4,6,5,3,1,0:T(2,128)(2,1)S(1)} %get-tuple-element.28), kind=kLoop, calls=%fused_computation.5 | loop fusion | flops 102400 | bytes 409600 | tf_op jit(solution)/shard_map/transpose | solution.py:384
  6.7 0.0 copy-start.2
  6.7 0.3 copy.51
  7.0 0.8 %copy.54.a2_ref = bf16[25,64,64]{2,1,0:T(8,128)(2,1)S(1)} copy(bf16[25,64,64]{0,2,1:T(8,128)(2,1)S(1)} %bitcast.59) | data formatting | bytes 409600 | tf_op jit(solution)/shard_map/reshape | solution.py:386
  7.8 0.2 convert_element_type.58
  8.1 0.2 fusion.7
  8.3 1.1 %rev.9 = bf16[2,25,1,12,2,12]{1,4,5,3,2,0:T(2,128)(2,1)S(1)} reverse(bf16[2,25,1,12,2,12]{1,4,5,3,2,0:T(2,128)(2,1)S(1)} %get-tuple-element.25), dimensions={4} | reverse | bytes 57600 | tf_op jit(solution)/shard_map/rev | solution.py:379
  9.4 0.5 maximum_bitcast_fusion.10
  9.9 0.6 fusion.4
  10.5 1.4 %maximum_bitcast_fusion.6 = (bf16[1,2,25,2,2,16,16]{2,4,6,5,3,1,0:T(2,128)(2,1)S(1)}, bf16[1,2,25,2,2,16,16]{2,4,6,5,3,1,0:T(2,128)(2,1)S(1)}) fusion(bf16[1,25,2,2,16,16]{1,3,5,4,2,0:T(2,128)(2,1)S(1)} %get-tuple-element.9, bf16[1,25,2,2,16,16]{1,3,5,4,2,0:T(2,128)(2,1)S(1)} %get-tuple-element.23, bf16[1,25,2,2,16,16]{1,3,5,4,2,0:T(2,128)(2,1)S(1)} %get-tuple-element.10), kind=kLoop, calls=%fused_computation.14 | loop fusion | flops 102400 | bytes 358400 | tf_op jit(solution)/shard_map/stack | solution.py:383
  11.9 1.8 %maximum_bitcast_fusion.1 = bf16[25,2,2,16,2,2,16]{0,4,6,3,1,5,2:T(2,128)(2,1)S(1)} fusion(bf16[1,2,25,2,2,16,16]{2,4,6,5,3,1,0:T(2,128)(2,1)S(1)} %get-tuple-element.31, bf16[1,2,25,2,2,16,16]{2,4,6,5,3,1,0:T(2,128)(2,1)S(1)} %get-tuple-element.30), kind=kLoop, calls=%fused_computation.4 | loop fusion | flops 102400 | bytes 409600 | tf_op jit(solution)/shard_map/transpose | solution.py:384
  13.7 0.3 copy.50
  14.0 0.8 %copy.53.a1_ref = bf16[25,64,64]{2,1,0:T(8,128)(2,1)S(1)} copy(bf16[25,64,64]{0,2,1:T(8,128)(2,1)S(1)} %bitcast.60) | data formatting | bytes 409600 | tf_op jit(solution)/shard_map/reshape | solution.py:386
  14.8 2.2 %copy.65 = bf16[8,2,12,25,25]{4,0,3,2,1:T(8,128)(2,1)S(1)} copy(f32[8,2,12,25,25]{4,1,3,2,0:T(2,128)} %param.20) | data formatting | bytes 720000 | tf_op args[6]
  17.0 0.3 copy.67
  17.3 0.3 slice_bitcast_fusion
  17.6 0.4 pad_negate_fusion.1
  18.0 0.2 pad.34
  18.2 0.9 %maximum_maximum_fusion.f_ref = bf16[12,8,64,64]{3,2,1,0:T(8,128)(2,1)S(1)} fusion(bf16[12,8,32,32]{3,2,1,0:T(8,128)(2,1)S(1)} %pad.34, bf16[12,8,32,32]{3,2,1,0:T(8,128)(2,1)S(1)} %get-tuple-element.14, bf16[12,8,32,32]{3,2,1,0:T(8,128)(2,1)S(1)} %get-tuple-element.13), kind=kLoop, calls=%fused_computation.2 | loop fusion | flops 3145728 | bytes 1376256 | tf_op jit(solution)/shard_map/concatenate | solution.py:372
  19.1 3.2 %reshape.65 = bf16[12,2,25,512]{3,1,2,0:T(2,128)(2,1)S(1)} reshape(bf16[12,2,25,2,4,64]{5,4,3,1,2,0:T(4,128)(2,1)} %bitcast.62) | data formatting | bytes 1228800 | tf_op jit(solution)/shard_map/reshape | solution.py:421
  22.3 0.0 copy-start.6
  22.3 0.0 copy-start.7
  22.4 0.0 copy-start.8
  22.4 0.0 copy-start
  22.4 0.1 copy.47
  22.5 0.1 pad.33
  22.6 0.4 copy-done.6
  23.0 0.0 copy-done.7
  23.0 0.0 copy-done.8
  23.0 0.1 select_reduce_fusion
  23.8 0.2 reshape.72.code_ref
  24.0 0.0 copy-done
  24.0 0.0 copy-start.1
  24.0 3.9 %shard_map.136.packed_ref = f32[48,128]{1,0:T(8,128)S(1)} custom-call(s32[2]{0:T(128)S(1)} %copy-done, bf16[768,512]{1,0:T(8,128)(2,1)S(1)} %bitcast.57, s32[512,1]{1,0:T(8,128)S(1)} %reshape.72.code_ref, bf16[12,8,64,64]{3,2,1,0:T(8,128)(2,1)S(1)} %maximum_maximum_fusion.f_ref, bf16[25,64,64]{2,1,0:T(8,128)(2,1)S(1)} %copy.53.a1_ref, ...), custom_call_target="tpu_custom_call" | custom-call | tf_op jit(solution)/shard_map/pallas_call | solution.py:429
  28.0 0.4 convert_bitcast_fusion
  28.4 0.4 fusion.5
  28.8 1.5 %rev.11 = bf16[2,25,1,32,2,12]{3,4,5,2,1,0:T(2,128)(2,1)S(1)} reverse(bf16[2,25,1,32,2,12]{3,4,5,2,1,0:T(2,128)(2,1)S(1)} %get-tuple-element.17), dimensions={4} | reverse | bytes 153600 | tf_op jit(solution)/shard_map/rev | solution.py:379
  30.3 1.0 %maximum_bitcast_fusion.5 = bf16[2,25,2,2,32,12]{4,3,5,2,1,0:T(2,128)(2,1)S(1)} fusion(bf16[2,25,1,32,2,12]{3,4,5,2,1,0:T(2,128)(2,1)S(1)} %rev.11, bf16[2,25,1,32,2,12]{3,4,5,2,1,0:T(2,128)(2,1)S(1)} %get-tuple-element.16), kind=kLoop, calls=%fused_computation.10 | loop fusion | flops 76800 | bytes 307200 | tf_op jit(solution)/shard_map/transpose | solution.py:380
  31.3 1.0 %fusion.2 = (bf16[1,25,2,2,32,16]{4,3,5,2,1,0:T(2,128)(2,1)S(1)}, bf16[1,25,2,2,32,16]{4,3,5,2,1,0:T(2,128)(2,1)S(1)}, bf16[1,25,2,2,32,16]{4,3,5,2,1,0:T(2,128)(2,1)S(1)}) fusion(bf16[2,25,2,2,32,12]{4,3,5,2,1,0:T(2,128)(2,1)S(1)} %maximum_bitcast_fusion.5), kind=kLoop, calls=%fused_computation.46 | loop fusion | flops 51200 | bytes 460800 | tf_op jit(solution)/shard_map/neg | solution.py:383
  32.3 2.4 %maximum_bitcast_fusion.3 = (bf16[1,2,25,2,2,32,16]{5,4,6,3,2,1,0:T(2,128)(2,1)S(1)}, bf16[1,2,25,2,2,32,16]{5,4,6,3,2,1,0:T(2,128)(2,1)S(1)}) fusion(bf16[1,25,2,2,32,16]{4,3,5,2,1,0:T(2,128)(2,1)S(1)} %get-tuple-element.5, bf16[1,25,2,2,32,16]{4,3,5,2,1,0:T(2,128)(2,1)S(1)} %get-tuple-element.15, bf16[1,25,2,2,32,16]{4,3,5,2,1,0:T(2,128)(2,1)S(1)} %get-tuple-element.6), kind=kLoop, calls=%fused_computation.6 | loop fusion | flops 204800 | bytes 716800 | tf_op jit(solution)/shard_map/stack | solution.py:383
  34.8 2.7 %maximum_bitcast_fusion = bf16[25,2,2,32,2,2,16]{3,4,6,1,0,5,2:T(2,128)(2,1)S(1)} fusion(bf16[1,2,25,2,2,32,16]{5,4,6,3,2,1,0:T(2,128)(2,1)S(1)} %get-tuple-element.19, bf16[1,2,25,2,2,32,16]{5,4,6,3,2,1,0:T(2,128)(2,1)S(1)} %get-tuple-element.18), kind=kLoop, calls=%fused_computation.1 | loop fusion | flops 204800 | bytes 819200 | tf_op jit(solution)/shard_map/transpose | solution.py:384
  37.5 1.7 %copy.56 = bf16[25,2,2,32,2,2,16]{3,2,1,6,5,4,0:T(2,128)(2,1)S(1)} copy(bf16[25,2,2,32,2,2,16]{3,4,6,1,0,5,2:T(2,128)(2,1)S(1)} %maximum_bitcast_fusion) | data formatting | bytes 819200 | tf_op jit(solution)/shard_map/transpose | solution.py:384
  39.2 0.0 copy-start.9
  39.3 0.0 copy-start.4
  39.3 0.8 %reshape.70 = bf16[25,128,64]{1,2,0:T(8,128)(2,1)S(1)} reshape(bf16[25,2,2,32,2,2,16]{3,2,1,6,5,4,0:T(2,128)(2,1)S(1)} %copy.56) | data formatting | bytes 819200 | tf_op jit(solution)/shard_map/reshape | solution.py:386
  40.1 0.0 copy-start.5
  40.1 0.4 copy.58.ao_ref
  40.6 0.0 copy-start.3
  40.6 0.0 copy-done.9
  40.6 0.6 dynamic_slice.3
  41.2 0.7 %fusion = (f32[256]{0:T(256)S(1)}, f32[256]{0:T(256)S(1)}) fusion(f32[]{:T(128)} %bitcast.23), kind=kLoop, calls=%fused_computation.38 | loop fusion | flops 768 | bytes 2052 | tf_op jit(solution)/shard_map/sin | solution.py:450
  41.9 0.1 broadcast_multiply_fusion.sin_ref
  42.1 0.1 maximum_maximum_fusion.1.fo_ref
  42.3 0.1 maximum_convert_fusion.ang_ref
  42.4 0.0 copy-done.3
  42.4 0.2 copy.68
  42.7 24.7 %shard_map.137 = f32[16,2048]{1,0:T(8,128)S(1)} custom-call(f32[48,128]{1,0:T(8,128)S(1)} %shard_map.136.packed_ref, bf16[12,64,64]{2,1,0:T(8,128)(2,1)S(1)} %maximum_maximum_fusion.1.fo_ref, bf16[25,128,64]{2,1,0:T(8,128)(2,1)S(1)} %copy.58.ao_ref, f32[8,256]{1,0:T(8,128)S(1)} %broadcast_in_dim.45.cos_ref, f32[8,256]{1,0:T(8,128)S(1)} %broadcast_multiply_fusion.sin_ref, ...), custom_call_target="tpu_custom_call" | custom-call | tf_op jit(solution)/shard_map/pallas_call | solution.py:458
  67.5 0.8 %copy.69 = f32[2,2,4,2048]{3,1,0,2:T(2,128)} copy(f32[2,2,4,2048]{3,2,1,0:T(4,128)S(1)} %reshape.71) | data formatting | bytes 262144 | tf_op jit(solution)/shard_map/reshape | solution.py:486
  (16 shorter events, 0.3 us)
Async XLA Ops:
  6.7 1.1 %copy-start.2 = (f32[2,25,2,12,2,12]{1,4,5,3,2,0:T(2,128)S(1)}, f32[2,25,2,12,2,12]{1,4,5,3,2,0:T(2,128)}, u32[]{:S(2)}) copy-start(f32[2,25,2,12,2,12]{1,4,5,3,2,0:T(2,128)} %param.21) | copy-start | bytes 345604
  22.3 0.7 copy-start.6
  22.3 0.7 copy-start.7
  22.4 0.7 copy-start.8
  22.4 1.6 %copy-start = (s32[2]{0:T(128)S(1)}, s32[2]{0:T(128)}, u32[]{:S(2)}) copy-start(s32[2]{0:T(128)} %box_ref.1) | copy-start | bytes 28
  24.0 4.0 %copy-start.1 = (f32[1,2,25,2,32,2,12]{4,5,6,3,2,1,0:T(2,128)S(1)}, f32[1,2,25,2,32,2,12]{4,5,6,3,2,1,0:T(2,128)}, u32[]{:S(2)}) copy-start(f32[1,2,25,2,32,2,12]{4,5,6,3,2,1,0:T(2,128)} %param.24) | copy-start | bytes 921604
  39.2 1.3 %copy-start.9 = (f32[4]{0:T(128)S(1)}, f32[4]{0:T(128)}, u32[]{:S(2)}) copy-start(f32[4]{0:T(128)} %param.25) | copy-start | bytes 52
  39.3 2.7 %copy-start.4 = (f32[1,2,12,25,25]{4,1,3,2,0:T(2,128)S(1)}, f32[1,2,12,25,25]{4,1,3,2,0:T(2,128)}, u32[]{:S(2)}) copy-start(f32[1,2,12,25,25]{4,1,3,2,0:T(2,128)} %param.23) | copy-start | bytes 180004
  40.1 2.1 %copy-start.5 = (bf16[64,32,32]{0,2,1:T(8,128)(2,1)S(1)}, bf16[64,32,32]{0,2,1:T(8,128)(2,1)}, u32[]{:S(2)}) copy-start(bf16[64,32,32]{0,2,1:T(8,128)(2,1)} %param.27) | copy-start | bytes 393220
  40.6 1.8 %copy-start.3 = (bf16[1,32,25,256]{3,1,2,0:T(8,128)(2,1)S(1)}, bf16[1,32,25,256]{3,1,2,0:T(8,128)(2,1)}, u32[]{:S(2)}) copy-start(bf16[1,32,25,256]{3,1,2,0:T(8,128)(2,1)} %param.26) | copy-start | bytes 1228804

commit v2 on v1

--- a/solution.py
+++ b/solution.py
@@ -32,25 +32,70 @@
 
 
 def axial_operand(y_ref, q):
-    pieces = [y_ref[pl.ds(part * QP + q, LP, stride=2 * QP), :] for part in range(2)]
-    here = jnp.concatenate(pieces, axis=0)
-    there = pltpu.roll(here, 64, 1)
-    return jnp.concatenate([here, there], axis=0).astype(jnp.bfloat16)
-
-
-def axial_pass(y_ref, z_ref, a_ref, orders):
     lane, _ = lane_ids()
     low = lane < 64
+    real, imag = [y_ref[pl.ds(part * QP + q, LP, stride=2 * QP), :] for part in range(2)]
+    real_turned = pltpu.roll(real, 64, 1)
+    imag_turned = pltpu.roll(imag, 64, 1)
+    return jnp.concatenate(
+        [
+            jnp.where(low, real, imag_turned),
+            jnp.where(low, real_turned, imag),
+            jnp.where(low, -imag, real_turned),
+            jnp.where(low, -imag_turned, real),
+        ],
+        axis=0,
+    ).astype(jnp.bfloat16)
+
+
+def axial_result(r):
+    lane, _ = lane_ids()
+    low = lane < 64
+    half = r.shape[0] // 2
+    first, second = r[:half], r[half:]
+    real = jnp.where(low, first, pltpu.roll(second, 64, 1))
+    imag = jnp.where(low, pltpu.roll(first, 64, 1), second)
+    return real, imag
+
+
+def identity(rows):
+    row = lax.broadcasted_iota(jnp.int32, (rows, 128), 0)
+    col = lax.broadcasted_iota(jnp.int32, (rows, 128), 1)
+    return jnp.where(row == col, 1.0, 0.0).astype(jnp.bfloat16)
+
+
+def dot_nt(a, b):
+    return lax.dot_general(a, b, (((1,), (1,)), ((), ())), preferred_element_type=jnp.float32)
+
+
+def axial_matrices(s_ref, a_ref, degrees):
+    eye = identity(QP)
+    zeros = jnp.zeros((64, 128), jnp.float32)
+    for u in range(2):
+        for w in range(degrees):
+            pieces = []
+            for part in range(2):
+                base = ((part * 2 + u) * degrees + w) * degrees * 2
+                for t in range(2):
+                    pieces.append(s_ref[pl.ds(base + t, LP, stride=2), :])
+            block = jnp.concatenate(pieces + [zeros], axis=0).astype(jnp.bfloat16)
+            a_ref[pl.ds(u * LP + w, QP, stride=2 * LP), :] = dot_nt(eye, block)
+
+
+def axial_pass(y_ref, z_ref, a_ref, orders):
     for q in range(orders):
-        r = dot(a_ref[q], axial_operand(y_ref, q))
-        z = jnp.where(low, r[: 2 * LP], r[2 * LP :])
-        for part in range(2):
-            z_ref[pl.ds(part * QP + q, LP, stride=2 * QP), :] = z[part * LP : (part + 1) * LP]
-
-
-def local_kernel(box_ref, xs_ref, code_ref, f_ref, a1_ref, a2_ref, out_ref, v_ref, y_ref, z_ref):
+        mats = a_ref[q * 2 * LP : (q + 1) * 2 * LP, :][:, :64].astype(jnp.bfloat16)
+        for part, z in enumerate(axial_result(dot(mats, axial_operand(y_ref, q)))):
+            z_ref[pl.ds(part * QP + q, LP, stride=2 * QP), :] = z
+
+
+def local_kernel(
+    orders, box_ref, xs_ref, code_ref, f_ref, s1_ref, s2_ref, out_ref, v_ref, y_ref, z_ref, a1_ref, a2_ref
+):
     degrees = f_ref.shape[0]
-    orders = a1_ref.shape[0]
+    for s_ref, a_ref in ((s1_ref, a1_ref), (s2_ref, a2_ref)):
+        a_ref[...] = jnp.zeros_like(a_ref)
+        axial_matrices(s_ref, a_ref, degrees)
     lane, rep = lane_ids()
     width = 2 * QP
     y_ref[...] = jnp.zeros_like(y_ref)
@@ -136,13 +181,13 @@
     dims,
     packed_ref,
     fo_ref,
-    ao_ref,
-    cos_ref,
-    sin_ref,
+    so_ref,
+    angle_ref,
     turn_ref,
     ang_ref,
     out_ref,
     recv1,
+    ao_ref,
     y_ref,
     zq_ref,
     vals_ref,
@@ -208,7 +253,28 @@
 
     y_ref[...] = jnp.zeros_like(y_ref)
     zq_ref[...] = jnp.zeros_like(zq_ref)
-    make_tables(tab_c, tab_s)
+    eye = identity(2 * nloc)
+    for q in range(q_orders):
+        pieces = []
+        for part in range(2):
+            for t in range(2):
+                first, second = [
+                    so_ref[
+                        pl.ds(((part * q_orders + q) * 2 + u) * degrees * 2 + t, LP, stride=2), :
+                    ]
+                    for u in range(2)
+                ]
+                pieces.append(first + pltpu.roll(second, nloc, 1))
+        ao_ref[q] = dot_nt(eye, jnp.concatenate(pieces, axis=0).astype(jnp.bfloat16)).astype(
+            jnp.bfloat16
+        )
+    azimuth = angle_ref[my_leaf]
+    order_values = (
+        lax.broadcasted_iota(jnp.int32, (8, orders), 1) - orders // 2
+    ).astype(jnp.float32)
+    cosine = jnp.cos(order_values * azimuth)
+    sine = jnp.sin(order_values * azimuth)
+    sine = jnp.where(lax.broadcasted_iota(jnp.int32, (8, orders), 0) < 4, sine, -sine)
 
     for copy in copies:
         copy.wait()
@@ -224,13 +290,10 @@
             fo_ref[l], vectors[l * width : (l + 1) * width]
         )
     for q in range(q_orders):
-        r = dot(ao_ref[q], axial_operand(y_ref, q))
-        zq_ref[q * 2 * nloc : (q + 1) * 2 * nloc, :] = jnp.where(
-            low, r[: 2 * nloc], r[2 * nloc :]
-        )
-
-    cosine = cos_ref[...]
-    sine = sin_ref[...]
+        for part, z in enumerate(axial_result(dot(ao_ref[q], axial_operand(y_ref, q)))):
+            start = (q * 2 + part) * nloc
+            zq_ref[start : start + nloc, :] = z
+
     for block in range(nloc // 8):
         gathered = jnp.zeros((QP, 128), jnp.float32)
         for n8 in range(8):
@@ -275,6 +338,7 @@
         )
         copy.start()
         copies.append(copy)
+    make_tables(tab_c, tab_s)
     for copy in copies:
         copy.wait()
     root = sbuf[my_leaf].astype(jnp.float32)
@@ -374,16 +438,9 @@
     )
 
 
-def axial_blocks(axial, out_rows):
-    mats = axial.astype(jnp.bfloat16)
-    mats = jnp.stack([mats[:, :, 0], mats[:, :, 1, :, ::-1]], axis=2)
-    mats = jnp.transpose(mats, (0, 1, 2, 4, 3, 5))
-    mats = pad_last(mats, out_rows, LP)
-    real, imag = mats[0], mats[1]
-    blocks = jnp.stack([jnp.stack([real, -imag], 0), jnp.stack([imag, real], 0)], 0)
-    blocks = jnp.transpose(blocks, (2, 3, 0, 5, 4, 1, 6))
-    orders = axial.shape[1]
-    return blocks.reshape(orders, 4 * out_rows, 4 * LP)
+def axial_rows(mats):
+    mats = mats.reshape(-1, mats.shape[-1])
+    return jnp.pad(mats, ((0, 16), (0, 128 - mats.shape[1])))
 
 
 def on_device(
@@ -422,12 +479,12 @@
     xs = pad_last(xs, QP, 8 * slots).reshape(degrees * 2 * QP, 8 * slots)
     turns = jnp.transpose(rotation, (1, 2, 0, 3, 4))
     f = rotation_blocks(turns[0], turns[1])
-    a1 = axial_blocks(axial_one, LP)
-    a2 = axial_blocks(axial_two, LP)
+    s1 = axial_rows(jnp.transpose(axial_one, (0, 2, 3, 5, 4, 1)))
+    s2 = axial_rows(jnp.transpose(axial_two, (0, 2, 3, 5, 4, 1)))
     rows = degrees * 2 * QP
     vmem = pl.BlockSpec(memory_space=pltpu.VMEM)
     packed = pl.pallas_call(
-        local_kernel,
+        functools.partial(local_kernel, morders),
         out_shape=jax.ShapeDtypeStruct((rows // 16, 128), f32),
         in_specs=[pl.BlockSpec(memory_space=pltpu.SMEM)] + [vmem] * 5,
         out_specs=vmem,
@@ -435,19 +492,16 @@
             pltpu.VMEM((rows, 128), bf16),
             pltpu.VMEM((LP * 2 * QP, 128), f32),
             pltpu.VMEM((LP * 2 * QP, 128), f32),
+            pltpu.VMEM((QP * 2 * LP, 128), f32),
+            pltpu.VMEM((QP * 2 * LP, 128), f32),
         ],
         compiler_params=pltpu.CompilerParams(vmem_limit_bytes=32 * 1024 * 1024),
-    )(box_octant, xs, code, f, a1, a2)
+    )(box_octant, xs, code, f, s1, s2)
 
     fo = rotation_blocks(owner_rotation[0, 0], owner_rotation[0, 1])
     nloc = turn_table.shape[1]
     orders = turn_table.shape[3]
-    ao = axial_blocks(owner_axial[0], nloc)
-    azimuth = owner_angle[lax.axis_index("leaf")]
-    order_values = (jnp.arange(orders, dtype=jnp.int32) - orders // 2).astype(f32)
-    flip = jnp.where(jnp.arange(8) < 4, 1.0, -1.0).astype(f32)
-    cosine = jnp.broadcast_to(jnp.cos(order_values * azimuth)[None, :], (8, orders))
-    sine = flip[:, None] * jnp.sin(order_values * azimuth)[None, :]
+    so = axial_rows(jnp.transpose(owner_axial[0], (0, 1, 2, 5, 4, 3)))
     turn = pad_last(turn_table[0], QP, orders)
     own = angular_table.shape[0]
     ang = jnp.transpose(angular_table, (1, 2, 0)).reshape(2, nloc // 2, -1, own)
@@ -458,10 +512,11 @@
     out = pl.pallas_call(
         functools.partial(owner_kernel, dims),
         out_shape=jax.ShapeDtypeStruct((16, PHI), f32),
-        in_specs=[vmem] * 7,
+        in_specs=[vmem] * 3 + [pl.BlockSpec(memory_space=pltpu.SMEM)] + [vmem] * 2,
         out_specs=vmem,
         scratch_shapes=[
             pltpu.VMEM((group - 1, rows // 16, 128), f32),
+            pltpu.VMEM((morders, 2 * nloc, 64), bf16),
             pltpu.VMEM((LP * 2 * QP, 128), f32),
             pltpu.VMEM((QP * 2 * nloc, 128), f32),
             pltpu.VMEM((nloc, 16, orders), f32),
@@ -482,7 +537,7 @@
         compiler_params=pltpu.CompilerParams(
             collective_id=0, has_side_effects=True, vmem_limit_bytes=48 * 1024 * 1024
         ),
-    )(packed, fo, ao, cosine, sine, turn, ang)
+    )(packed, fo, so, owner_angle, turn, ang)
     out = out.reshape(2, 2, 4, PHI)
     return jnp.transpose(out, (2, 0, 1, 3))[None]
 

time: 68.5 us -> 44.7 us (0.65)
  other arithmetic: 20 us -> 1.65 us
  local copies, waits for them, and re-layouts: 18.5 us -> 12.2 us
  Pallas kernels: 28.7 us -> 29.6 us
    transpose x6 -> x0, other arithmetic: 8.2 us -> none  [the longest x3 6.24 us: axial_blocks(): blocks = jnp.transpose(blocks, (2, 3, 0, 5, 4, 1, 6))]
    another operation x3 -> x0, other arithmetic: 5.28 us -> none  [axial_blocks(): jnp.stack([jnp.stack([real, -imag], 0), jnp.stack([imag, real], 0)], 0)]
    unnamed x23 -> x29, local copies, waits for them, and re-layouts: 2.9 us -> 7.33 us
    rev x3 -> x0, local copies, waits for them, and re-layouts: 3.59 us -> none  [axial_blocks(): mats = jnp.stack([mats[:, :, 0], mats[:, :, 1, :, ::-1]], axis=2)]
    reshape x4 -> x0, local copies, waits for them, and re-layouts: 2.94 us -> none  [axial_blocks(): return blocks.reshape(orders, 4 * out_rows, 4 * LP)]
    reshape x2, local copies, waits for them, and re-layouts: 3.36 us -> 0.75 us  [on_device(): jnp.transpose(sphere_coef, (0, 2, 1, 3, 4, 5))]
    transpose x3 -> x0, local copies, waits for them, and re-layouts: 2.24 us -> none  [axial_blocks(): blocks = jnp.transpose(blocks, (2, 3, 0, 5, 4, 1, 6))]
    neg x3 -> x0, other arithmetic: 2.19 us -> none  [axial_blocks(): -imag]
where the time goes in v2:
time: 44.7 us; the launch traced here: 44.4 us
  Pallas kernels  29.6 us (66%)
  local copies, waits for them, and re-layouts  12.2 us (27%)
  other arithmetic  1.65 us (4%)
  between operations  0.93 us (2%)
    pallas_call x1, Pallas kernels, on_device(): pl.pallas_call(functools.partial(owner_kernel, dims), out_shape=jax.Shape...  25.3 us
    unnamed x29, local copies, waits for them, and re-layouts  7.33 us
    pallas_call x1, Pallas kernels, on_device(): pl.pallas_call(functools.partial(local_kernel, morders), out_shape=jax.Sh...  4.26 us
    reshape x1, local copies, waits for them, and re-layouts, on_device(): code = jnp.broadcast_to(code[None, :], (8, slots)).reshape(8 * slots, 1)  1.59 us
    concatenate x2, other arithmetic, rotation_blocks(): jnp.concatenate([jnp.concatenate([real, -imag], -1), jnp.concatenate([ima...  1 us

profile of v2, /device:TPU:0, one launch (start us, length us, event | category | flops | bytes accessed | tf_op | source)
XLA Modules:
  0.0 44.4 jit_solution(2031068301297865398)
XLA Ops:
  0.0 2.2 %copy.44 = bf16[8,2,12,25,25]{4,0,3,2,1:T(8,128)(2,1)S(1)} copy(f32[8,2,12,25,25]{4,1,3,2,0:T(2,128)} %param.20) | data formatting | bytes 720000 | tf_op args[6]
  2.2 0.3 copy.46
  2.5 0.3 slice_bitcast_fusion
  2.8 0.4 pad_negate_fusion.1
  3.2 0.2 pad.34
  3.4 0.0 copy-start.3
  3.4 0.9 %maximum_maximum_fusion.f_ref = bf16[12,8,64,64]{3,2,1,0:T(8,128)(2,1)S(1)} fusion(bf16[12,8,32,32]{3,2,1,0:T(8,128)(2,1)S(1)} %pad.34, bf16[12,8,32,32]{3,2,1,0:T(8,128)(2,1)S(1)} %get-tuple-element.8, bf16[12,8,32,32]{3,2,1,0:T(8,128)(2,1)S(1)} %get-tuple-element.7), kind=kLoop, calls=%fused_computation.1 | loop fusion | flops 3145728 | bytes 1376256 | tf_op jit(solution)/shard_map/concatenate | solution.py:436
  4.3 0.4 copy-done.3
  4.7 0.6 %reshape.49 = bf16[12,2,25,512]{3,1,2,0:T(2,128)(2,1)S(1)} reshape(bf16[12,2,25,2,4,64]{5,4,3,1,2,0:T(4,128)(2,1)S(1)} %bitcast.40) | data formatting | bytes 1228800 | tf_op jit(solution)/shard_map/reshape | solution.py:478
  5.3 0.0 copy-start.5
  5.3 0.1 copy.32
  5.5 0.0 copy-start.6
  5.5 0.1 pad.33
  5.6 0.0 copy-start.10
  5.6 0.0 copy-start.11
  5.6 0.0 copy-start.12
  5.6 0.8 %copy-done.5 = f32[2,25,2,12,2,12]{1,4,5,3,2,0:T(2,128)S(1)} copy-done((f32[2,25,2,12,2,12]{1,4,5,3,2,0:T(2,128)S(1)}, f32[2,25,2,12,2,12]{1,4,5,3,2,0:T(2,128)}, u32[]{:S(2)}) %copy-start.5) | copy-done | bytes 115224
  6.4 0.2 copy-done.6
  6.7 0.0 copy-done.10
  6.7 0.0 copy-done.11
  6.7 0.0 copy-done.12
  6.7 0.1 select_reduce_fusion
  7.5 0.6 %broadcast_in_dim.28 = s32[8,64]{1,0:T(8,128)} broadcast(s32[64]{0:T(128)S(1)} %compare_select_fusion), dimensions={1} | broadcast | bytes 2304 | tf_op jit(solution)/shard_map/broadcast_in_dim | solution.py:476
  8.1 1.6 %reshape.56.code_ref = s32[512,1]{1,0:T(8,128)} reshape(s32[8,64]{1,0:T(8,128)} %broadcast_in_dim.28) | data formatting | bytes 4096 | tf_op jit(solution)/shard_map/reshape | solution.py:476
  9.6 0.0 copy-start
  9.6 0.9 %copy-done = s32[512,1]{1,0:T(8,128)S(1)} copy-done((s32[512,1]{1,0:T(8,128)S(1)}, s32[512,1]{1,0:T(8,128)}, u32[]{:S(2)}) %copy-start) | copy-done | bytes 2072
  10.6 0.0 copy-start.1
  10.6 0.7 %copy-done.1 = s32[2]{0:T(128)S(1)} copy-done((s32[2]{0:T(128)S(1)}, s32[2]{0:T(128)}, u32[]{:S(2)}) %copy-start.1) | copy-done | bytes 32
  11.2 0.0 copy-start.8
  11.2 4.3 %shard_map.136.packed_ref = f32[48,128]{1,0:T(8,128)S(1)} custom-call(s32[2]{0:T(128)S(1)} %copy-done.1, bf16[768,512]{1,0:T(8,128)(2,1)S(1)} %bitcast.37, s32[512,1]{1,0:T(8,128)S(1)} %copy-done, bf16[12,8,64,64]{3,2,1,0:T(8,128)(2,1)S(1)} %maximum_maximum_fusion.f_ref, f32[1168,128]{1,0:T(8,128)S(1)} %pad.36.s1_ref, f32[1168,128]{1,0:T(8,128)S(1)} %pad.37.s2_ref), custom_call_target="tpu_custom_call" | custom-call | tf_op jit(solution)/shard_map/pallas_call | solution.py:486
  15.5 0.0 copy-done.8
  15.5 0.0 copy-start.9
  15.5 0.0 copy-start.4
  15.7 0.1 maximum_maximum_fusion.1.fo_ref
  15.8 0.6 %copy-done.9 = bf16[64,32,32]{0,2,1:T(8,128)(2,1)S(1)} copy-done((bf16[64,32,32]{0,2,1:T(8,128)(2,1)S(1)}, bf16[64,32,32]{0,2,1:T(8,128)(2,1)}, u32[]{:S(2)}) %copy-start.9) | copy-done | bytes 131096
  16.5 0.0 copy-start.7
  16.5 0.1 maximum_convert_fusion.ang_ref
  16.6 0.3 copy-done.4
  16.9 0.1 pad.40.so_ref
  17.0 0.6 %copy-done.7 = bf16[1,32,25,256]{3,1,2,0:T(8,128)(2,1)S(1)} copy-done((bf16[1,32,25,256]{3,1,2,0:T(8,128)(2,1)S(1)}, bf16[1,32,25,256]{3,1,2,0:T(8,128)(2,1)}, u32[]{:S(2)}) %copy-start.7) | copy-done | bytes 409624
  17.6 0.0 copy-start.2
  17.6 0.2 copy.47
  17.8 0.1 pad.41.turn_ref
  17.9 0.4 copy-done.2
  18.2 25.3 %shard_map.137 = f32[16,2048]{1,0:T(8,128)S(1)} custom-call(f32[48,128]{1,0:T(8,128)S(1)} %shard_map.136.packed_ref, bf16[12,64,64]{2,1,0:T(8,128)(2,1)S(1)} %maximum_maximum_fusion.1.fo_ref, f32[2416,128]{1,0:T(8,128)S(1)} %pad.40.so_ref, f32[4]{0:T(128)S(1)} %copy-done.2, bf16[32,32,256]{2,1,0:T(8,128)(2,1)S(1)} %pad.41.turn_ref, ...), custom_call_target="tpu_custom_call" | custom-call | tf_op jit(solution)/shard_map/pallas_call | solution.py:512
  43.6 0.8 %copy.48 = f32[2,2,4,2048]{3,1,0,2:T(2,128)} copy(f32[2,2,4,2048]{3,2,1,0:T(4,128)S(1)} %reshape.55) | data formatting | bytes 262144 | tf_op jit(solution)/shard_map/reshape | solution.py:541
  (10 shorter events, 0.3 us)
Async XLA Ops:
  3.4 1.3 %copy-start.3 = (bf16[12,25,2,2,4,64]{5,4,3,2,1,0:T(4,128)(2,1)S(1)}, bf16[12,25,2,2,4,64]{5,4,3,2,1,0:T(4,128)(2,1)}, u32[]{:S(2)}) copy-start(bf16[12,25,2,2,4,64]{5,4,3,2,1,0:T(4,128)(2,1)} %param.14) | copy-start | bytes 1843204
  5.3 1.1 %copy-start.5 = (f32[2,25,2,12,2,12]{1,4,5,3,2,0:T(2,128)S(1)}, f32[2,25,2,12,2,12]{1,4,5,3,2,0:T(2,128)}, u32[]{:S(2)}) copy-start(f32[2,25,2,12,2,12]{1,4,5,3,2,0:T(2,128)} %param.21) | copy-start | bytes 345604
  5.5 1.1 %copy-start.6 = (f32[2,25,2,12,2,12]{1,4,5,3,2,0:T(2,128)S(1)}, f32[2,25,2,12,2,12]{1,4,5,3,2,0:T(2,128)}, u32[]{:S(2)}) copy-start(f32[2,25,2,12,2,12]{1,4,5,3,2,0:T(2,128)} %param.22) | copy-start | bytes 345604
  5.6 1.1 %copy-start.10 = (s32[16]{0:T(128)S(1)}, s32[16]{0:T(128)}, u32[]{:S(2)}) copy-start(s32[16]{0:T(128)} %param.17) | copy-start | bytes 196
  5.6 1.1 %copy-start.11 = (s32[16]{0:T(128)S(1)}, s32[16]{0:T(128)}, u32[]{:S(2)}) copy-start(s32[16]{0:T(128)} %param.18) | copy-start | bytes 196
  5.6 1.1 %copy-start.12 = (s32[64]{0:T(128)S(1)}, s32[64]{0:T(128)}, u32[]{:S(2)}) copy-start(s32[64]{0:T(128)} %param.16) | copy-start | bytes 772
  9.6 0.9 %copy-start = (s32[512,1]{1,0:T(8,128)S(1)}, s32[512,1]{1,0:T(8,128)}, u32[]{:S(2)}) copy-start(s32[512,1]{1,0:T(8,128)} %reshape.56.code_ref) | copy-start | bytes 6148
  10.6 0.7 %copy-start.1 = (s32[2]{0:T(128)S(1)}, s32[2]{0:T(128)}, u32[]{:S(2)}) copy-start(s32[2]{0:T(128)} %box_ref.1) | copy-start | bytes 28
  11.2 4.3 %copy-start.8 = (f32[1,2,12,25,25]{4,1,3,2,0:T(2,128)S(1)}, f32[1,2,12,25,25]{4,1,3,2,0:T(2,128)}, u32[]{:S(2)}) copy-start(f32[1,2,12,25,25]{4,1,3,2,0:T(2,128)} %param.23) | copy-start | bytes 180004
  15.5 1.0 %copy-start.9 = (bf16[64,32,32]{0,2,1:T(8,128)(2,1)S(1)}, bf16[64,32,32]{0,2,1:T(8,128)(2,1)}, u32[]{:S(2)}) copy-start(bf16[64,32,32]{0,2,1:T(8,128)(2,1)} %param.27) | copy-start | bytes 393220
  15.5 1.4 %copy-start.4 = (f32[1,2,25,2,32,2,12]{4,5,6,3,2,1,0:T(2,128)S(1)}, f32[1,2,25,2,32,2,12]{4,5,6,3,2,1,0:T(2,128)}, u32[]{:S(2)}) copy-start(f32[1,2,25,2,32,2,12]{4,5,6,3,2,1,0:T(2,128)} %param.24) | copy-start | bytes 921604
  16.5 1.1 %copy-start.7 = (bf16[1,32,25,256]{3,1,2,0:T(8,128)(2,1)S(1)}, bf16[1,32,25,256]{3,1,2,0:T(8,128)(2,1)}, u32[]{:S(2)}) copy-start(bf16[1,32,25,256]{3,1,2,0:T(8,128)(2,1)} %param.26) | copy-start | bytes 1228804
  17.6 0.7 %copy-start.2 = (f32[4]{0:T(128)S(1)}, f32[4]{0:T(128)}, u32[]{:S(2)}) copy-start(f32[4]{0:T(128)} %angle_ref.1) | copy-start | bytes 52

commit v3 on v2

--- a/solution.py
+++ b/solution.py
@@ -82,6 +82,21 @@
             a_ref[pl.ds(u * LP + w, QP, stride=2 * LP), :] = dot_nt(eye, block)
 
 
+def rotation_matrices(w_ref, f_ref, orders):
+    degrees = f_ref.shape[0]
+
+    def body(l, carry):
+        for o in range(8):
+            base = (o * degrees + l) * orders * 2
+            real = w_ref[pl.ds(base, QP, stride=2), :]
+            imag = w_ref[pl.ds(base + 1, QP, stride=2), :]
+            f_ref[l, o, :QP, :] = (real - pltpu.roll(imag, QP, 1)).astype(jnp.bfloat16)
+            f_ref[l, o, QP:, :] = (imag + pltpu.roll(real, QP, 1)).astype(jnp.bfloat16)
+        return carry
+
+    lax.fori_loop(0, degrees, body, 0)
+
+
 def axial_pass(y_ref, z_ref, a_ref, orders):
     for q in range(orders):
         mats = a_ref[q * 2 * LP : (q + 1) * 2 * LP, :][:, :64].astype(jnp.bfloat16)
@@ -90,7 +105,23 @@
 
 
 def local_kernel(
-    orders, box_ref, xs_ref, code_ref, f_ref, s1_ref, s2_ref, out_ref, v_ref, y_ref, z_ref, a1_ref, a2_ref
+    orders,
+    box_ref,
+    live_ref,
+    octant_ref,
+    parent_ref,
+    xs_ref,
+    cluster_ref,
+    w_ref,
+    s1_ref,
+    s2_ref,
+    out_ref,
+    v_ref,
+    y_ref,
+    z_ref,
+    a1_ref,
+    a2_ref,
+    f_ref,
 ):
     degrees = f_ref.shape[0]
     for s_ref, a_ref in ((s1_ref, a1_ref), (s2_ref, a2_ref)):
@@ -100,14 +131,20 @@
     width = 2 * QP
     y_ref[...] = jnp.zeros_like(y_ref)
     z_ref[...] = jnp.zeros_like(z_ref)
+    rotation_matrices(w_ref, f_ref, orders)
     slots = xs_ref.shape[1] // 8
-    row = lax.broadcasted_iota(jnp.int32, (8 * slots, 128), 0) // slots
-    col = lax.broadcasted_iota(jnp.int32, (8 * slots, 128), 1)
-    keep = (
-        (row // 4 == col // 64) & (row % 4 == col % 4) & ((col % 64) // 4 == code_ref[...])
-    )
+    cluster = cluster_ref[...]
+    code = jnp.full((1, slots), -1, jnp.int32)
+    for leaf in range(octant_ref.shape[0]):
+        code = jnp.where(cluster == leaf, octant_ref[leaf] * 2 + parent_ref[leaf], code)
+    slot = lax.broadcasted_iota(jnp.int32, (1, slots), 1)
+    code = jnp.where(slot // (slots // SBLK) < live_ref[0], code, -1)
+    code = jnp.concatenate([code] * 8, axis=1)
+    row = lax.broadcasted_iota(jnp.int32, (128, 8 * slots), 0)
+    col = lax.broadcasted_iota(jnp.int32, (128, 8 * slots), 1) // slots
+    keep = (row // 64 == col // 4) & (row % 4 == col % 4) & ((row % 64) // 4 == code)
     spread = jnp.where(keep, 1.0, 0.0).astype(jnp.bfloat16)
-    v_ref[...] = dot(xs_ref[...], spread).astype(jnp.bfloat16)
+    v_ref[...] = dot_nt(xs_ref[...], spread).astype(jnp.bfloat16)
     octant = rep // 2
     box = rep % 2
 
@@ -115,22 +152,22 @@
         for l in range(degrees):
             v = v_ref[l * width : (l + 1) * width, :]
             if level == 0:
-                r = dot(f_ref[l].reshape(8 * width, width), v)
+                r = dot(f_ref[l].reshape(8 * width, 128)[:, :width], v)
                 acc = r[:width]
                 for o in range(1, 8):
                     acc = jnp.where(octant == o, r[o * width : (o + 1) * width], acc)
             else:
-                acc = dot(f_ref[l, box_ref[0]], v)
-                acc = jnp.where(box == 1, dot(f_ref[l, box_ref[1]], v), acc)
+                acc = dot(f_ref[l, box_ref[0]][:, :width], v)
+                acc = jnp.where(box == 1, dot(f_ref[l, box_ref[1]][:, :width], v), acc)
             y_ref[l * width : (l + 1) * width, :] = acc
         axial_pass(y_ref, z_ref, a1_ref if level == 0 else a2_ref, orders)
         for l in range(degrees):
             z = z_ref[l * width : (l + 1) * width, :]
             if level == 0:
-                mats = f_ref[l].reshape(8 * width, width)
+                mats = f_ref[l].reshape(8 * width, 128)[:, :width]
                 parts = [jnp.where(octant == o, z, 0.0) for o in range(8)]
             else:
-                mats = jnp.concatenate([f_ref[l, box_ref[0]], f_ref[l, box_ref[1]]], axis=0)
+                mats = jnp.concatenate([f_ref[l, box_ref[b]][:, :width] for b in range(2)], axis=0)
                 parts = [jnp.where(box == b, z, 0.0) for b in range(2)]
             stacked = jnp.concatenate(parts, axis=0).astype(jnp.bfloat16)
             r = lax.dot_general(
@@ -153,21 +190,28 @@
     out_ref[...] = packed
 
 
+def circle(steps):
+    steps = jnp.bitwise_and(steps + PHI // 2, PHI - 1) - PHI // 2
+    x = steps.astype(jnp.float32) * (0.5 * math.pi / PHI)
+    x2 = x * x
+    sine = x * (1 + x2 * (-1 / 6 + x2 * (1 / 120 + x2 * (-1 / 5040 + x2 * (1 / 362880)))))
+    cosine = 1 + x2 * (-1 / 2 + x2 * (1 / 24 + x2 * (-1 / 720 + x2 * (1 / 40320))))
+    for _ in range(2):
+        sine, cosine = 2 * sine * cosine, 1 - 2 * sine * sine
+    return cosine, sine
+
+
 def make_tables(tab_c, tab_s):
     orders = tab_c.shape[0]
     j = lax.broadcasted_iota(jnp.int32, (16, 128), 0) - orders // 2
     k = lax.broadcasted_iota(jnp.int32, (16, 128), 1)
-    step = 2.0 * math.pi / PHI
     turns = []
     for a in range(PHI // 128):
-        angle = (jnp.bitwise_and(j * (128 * a), PHI - 1)).astype(jnp.float32) * step
-        turns.append((jnp.cos(angle), jnp.sin(angle)))
+        turns.append(circle(j * (128 * a)))
 
     def body(i, carry):
         r0 = pl.multiple_of(i * 16, 16)
-        angle = (jnp.bitwise_and((j + r0) * k, PHI - 1)).astype(jnp.float32) * step
-        c1 = jnp.cos(angle)
-        s1 = jnp.sin(angle)
+        c1, s1 = circle((j + r0) * k)
         for a, (c2, s2) in enumerate(turns):
             cols = slice(a * 128, (a + 1) * 128)
             tab_c[pl.ds(r0, 16), cols] = (c1 * c2 - s1 * s2).astype(jnp.bfloat16)
@@ -349,7 +393,18 @@
     lats = ang_ref.shape[1] // 2
     sign = jnp.where(lax.broadcasted_iota(jnp.int32, (8, 128), 0) < 4, -1.0, 1.0)
 
-    def latitude(h, carry):
+    def field_copy(d):
+        target = lax.rem(me + d, holders)
+        return pltpu.make_async_remote_copy(
+            src_ref=fbuf.at[target],
+            dst_ref=recv3.at[me],
+            send_sem=send3.at[d - 1],
+            recv_sem=rsem3.at[d - 1],
+            device_id=device(target),
+            device_id_type=MESH,
+        )
+
+    def latitude(h):
         theta = jnp.zeros((8, 128), jnp.float32)
         cross = jnp.zeros((8, 128), jnp.float32)
         for n in range(half):
@@ -363,22 +418,9 @@
         cross = cross + pltpu.roll(cross, 64, 1)
         phi = sign * pltpu.roll(cross, 4, 0)
         fbuf[h] = jnp.concatenate([theta, phi], axis=0).astype(jnp.bfloat16)
-        return carry
-
-    lax.fori_loop(0, lats, latitude, 0)
-
-    def field_copy(d):
-        target = lax.rem(me + d, holders)
-        return pltpu.make_async_remote_copy(
-            src_ref=fbuf.at[target],
-            dst_ref=recv3.at[me],
-            send_sem=send3.at[d - 1],
-            recv_sem=rsem3.at[d - 1],
-            device_id=device(target),
-            device_id_type=MESH,
-        )
 
     def start(d, carry):
+        latitude(lax.rem(me + d, holders))
         field_copy(d).start()
         return carry
 
@@ -396,6 +438,7 @@
         return carry
 
     lax.fori_loop(1, holders, start, 0)
+    latitude(me)
     recv3[me] = fbuf[me]
     lax.fori_loop(1, holders, finish, 0)
 
@@ -468,17 +511,10 @@
     bf16 = jnp.bfloat16
     f32 = jnp.float32
 
-    leaf_code = leaf_octant * 2 + leaf_parent
-    member = cluster[:, None] == jnp.arange(leaf_code.shape[0], dtype=jnp.int32)[None, :]
-    code = jnp.sum(jnp.where(member, leaf_code[None, :], 0), axis=1)
-    alive = jnp.arange(slots, dtype=jnp.int32) // (slots // SBLK) < live_blocks[0]
-    code = jnp.where(alive, code, -1)
-    code = jnp.broadcast_to(code[None, :], (8, slots)).reshape(8 * slots, 1)
-
     xs = jnp.transpose(sphere_coef, (0, 2, 1, 3, 4, 5)).reshape(degrees, 2, morders, 8 * slots)
     xs = pad_last(xs, QP, 8 * slots).reshape(degrees * 2 * QP, 8 * slots)
-    turns = jnp.transpose(rotation, (1, 2, 0, 3, 4))
-    f = rotation_blocks(turns[0], turns[1])
+    w = jnp.transpose(rotation, (0, 2, 3, 1, 4)).reshape(-1, morders)
+    w = jnp.pad(w, ((0, 16), (0, 128 - morders)))
     s1 = axial_rows(jnp.transpose(axial_one, (0, 2, 3, 5, 4, 1)))
     s2 = axial_rows(jnp.transpose(axial_two, (0, 2, 3, 5, 4, 1)))
     rows = degrees * 2 * QP
@@ -486,7 +522,7 @@
     packed = pl.pallas_call(
         functools.partial(local_kernel, morders),
         out_shape=jax.ShapeDtypeStruct((rows // 16, 128), f32),
-        in_specs=[pl.BlockSpec(memory_space=pltpu.SMEM)] + [vmem] * 5,
+        in_specs=[pl.BlockSpec(memory_space=pltpu.SMEM)] * 4 + [vmem] * 5,
         out_specs=vmem,
         scratch_shapes=[
             pltpu.VMEM((rows, 128), bf16),
@@ -494,9 +530,20 @@
             pltpu.VMEM((LP * 2 * QP, 128), f32),
             pltpu.VMEM((QP * 2 * LP, 128), f32),
             pltpu.VMEM((QP * 2 * LP, 128), f32),
+            pltpu.VMEM((degrees, 8, 2 * QP, 128), bf16),
         ],
         compiler_params=pltpu.CompilerParams(vmem_limit_bytes=32 * 1024 * 1024),
-    )(box_octant, xs, code, f, s1, s2)
+    )(
+        box_octant,
+        live_blocks,
+        leaf_octant,
+        leaf_parent,
+        xs,
+        cluster.reshape(1, slots),
+        w,
+        s1,
+        s2,
+    )
 
     fo = rotation_blocks(owner_rotation[0, 0], owner_rotation[0, 1])
     nloc = turn_table.shape[1]

time: 44.7 us -> 40.4 us (0.904)
  local copies, waits for them, and re-layouts: 12.2 us -> 8.92 us
  other arithmetic: 1.65 us -> 0.28 us
    unnamed x29 -> x26, local copies, waits for them, and re-layouts: 7.33 us -> 4.47 us
    reshape x2, local copies, waits for them, and re-layouts: 0.75 us -> 3.14 us  [on_device(): jnp.transpose(sphere_coef, (0, 2, 1, 3, 4, 5))]
    pallas_call x1, Pallas kernels: 4.26 us -> 6.05 us  [on_device(): pl.pallas_call(functools.partial(local_kernel, morders), out_shape=jax.Sh...]
    reshape x1 -> x0, local copies, waits for them, and re-layouts: 1.59 us -> none  [on_device(): code = jnp.broadcast_to(code[None, :], (8, slots)).reshape(8 * slots, 1)]
    pallas_call x1, Pallas kernels: 25.3 us -> 24 us  [on_device(): pl.pallas_call(functools.partial(owner_kernel, dims), out_shape=jax.Shape...]
    concatenate x2 -> x1, other arithmetic: 1 us -> 0.13 us  [rotation_blocks(): jnp.concatenate([jnp.concatenate([real, -imag], -1), jnp.concatenate([ima...]
    broadcast_in_dim x1 -> x0, local copies, waits for them, and re-layouts: 0.6 us -> none  [on_device(): code = jnp.broadcast_to(code[None, :], (8, slots)).reshape(8 * slots, 1)]
where the time goes in v3:
time: 40.4 us; the launch traced here: 40.1 us
  Pallas kernels  30 us (74%)
  local copies, waits for them, and re-layouts  8.92 us (22%)
  between operations  0.9 us (2%)
    pallas_call x1, Pallas kernels, on_device(): pl.pallas_call(functools.partial(owner_kernel, dims), out_shape=jax.Shape...  24 us
    pallas_call x1, Pallas kernels, on_device(): pl.pallas_call(functools.partial(local_kernel, morders), out_shape=jax.Sh...  6.05 us
    unnamed x26, local copies, waits for them, and re-layouts  4.47 us
    reshape x2, local copies, waits for them, and re-layouts, on_device(): jnp.transpose(sphere_coef, (0, 2, 1, 3, 4, 5))  3.14 us

profile of v3, /device:TPU:0, one launch (start us, length us, event | category | flops | bytes accessed | tf_op | source)
XLA Modules:
  0.0 40.1 jit_solution(1040097755803240527)
XLA Ops:
  0.7 3.0 %reshape.31 = bf16[12,2,25,512]{3,1,2,0:T(2,128)(2,1)S(1)} reshape(bf16[12,2,25,2,4,64]{5,4,3,1,2,0:T(4,128)(2,1)} %bitcast.36) | data formatting | bytes 1228800 | tf_op jit(solution)/shard_map/reshape | solution.py:514
  3.7 0.0 copy-start.5
  3.7 0.1 copy.15
  3.8 0.1 pad.30
  3.9 1.4 %copy-done.5 = f32[8,2,12,25,25]{4,1,3,2,0:T(2,128)S(1)} copy-done((f32[8,2,12,25,25]{4,1,3,2,0:T(2,128)S(1)}, f32[8,2,12,25,25]{4,1,3,2,0:T(2,128)}, u32[]{:S(2)}) %copy-start.5) | copy-done | bytes 480024
  5.4 0.0 copy-start.7
  5.4 0.2 pad.31.w_ref
  5.5 0.0 copy-start.8
  5.5 0.0 copy-start
  5.5 0.0 copy-start.1
  5.6 0.0 copy-start.2
  5.6 0.0 copy-start.3
  5.6 0.8 %copy-done.7 = f32[2,25,2,12,2,12]{1,4,5,3,2,0:T(2,128)S(1)} copy-done((f32[2,25,2,12,2,12]{1,4,5,3,2,0:T(2,128)S(1)}, f32[2,25,2,12,2,12]{1,4,5,3,2,0:T(2,128)}, u32[]{:S(2)}) %copy-start.7) | copy-done | bytes 115224
  6.5 0.2 copy-done.8
  6.7 0.0 copy-done
  6.7 0.0 copy-done.1
  6.7 0.0 copy-done.2
  6.7 0.0 copy-done.3
  6.7 0.0 copy-start.10
  6.7 6.0 %shard_map.136.packed_ref = f32[48,128]{1,0:T(8,128)S(1)} custom-call(s32[2]{0:T(128)S(1)} %copy-done, s32[1]{0:T(128)S(6)} %copy.25.live_ref, s32[16]{0:T(128)S(1)} %copy-done.1, s32[16]{0:T(128)S(1)} %copy-done.2, bf16[768,512]{1,0:T(8,128)(2,1)S(1)} %bitcast.32, s32[1,64]{1,0:T(1,128)S(1)} %bitcast.33, f32[4816,128]{1,0:T(8,128)S(1)} %pad.31.w_ref, ...), custom_call_target="tpu_custom_call" | custom-call | tf_op jit(solution)/shard_map/pallas_call | solution.py:522
  12.8 0.0 copy-done.10
  12.8 0.0 copy-start.6
  13.0 0.1 maximum_maximum_fusion.fo_ref
  13.1 0.0 copy-start.9
  13.1 1.0 %copy-done.6 = f32[1,2,25,2,32,2,12]{4,5,6,3,2,1,0:T(2,128)S(1)} copy-done((f32[1,2,25,2,32,2,12]{4,5,6,3,2,1,0:T(2,128)S(1)}, f32[1,2,25,2,32,2,12]{4,5,6,3,2,1,0:T(2,128)}, u32[]{:S(2)}) %copy-start.6) | copy-done | bytes 307224
  14.1 0.1 pad.36.so_ref
  14.2 0.1 copy-done.9
  14.2 0.0 copy-start.11
  14.2 0.2 copy.23
  14.5 0.0 copy-start.4
  14.5 0.6 %copy-done.11 = bf16[64,32,32]{0,2,1:T(8,128)(2,1)S(1)} copy-done((bf16[64,32,32]{0,2,1:T(8,128)(2,1)S(1)}, bf16[64,32,32]{0,2,1:T(8,128)(2,1)}, u32[]{:S(2)}) %copy-start.11) | copy-done | bytes 131096
  15.2 0.1 maximum_convert_fusion.ang_ref
  15.3 0.0 copy-done.4
  15.3 24.0 %shard_map.137 = f32[16,2048]{1,0:T(8,128)S(1)} custom-call(f32[48,128]{1,0:T(8,128)S(1)} %shard_map.136.packed_ref, bf16[12,64,64]{2,1,0:T(8,128)(2,1)S(1)} %maximum_maximum_fusion.fo_ref, f32[2416,128]{1,0:T(8,128)S(1)} %pad.36.so_ref, f32[4]{0:T(128)S(1)} %copy-done.4, bf16[32,32,256]{2,1,0:T(8,128)(2,1)S(1)} %pad.37.turn_ref, ...), custom_call_target="tpu_custom_call" | custom-call | tf_op jit(solution)/shard_map/pallas_call | solution.py:559
  39.4 0.8 %copy.24 = f32[2,2,4,2048]{3,1,0,2:T(2,128)} copy(f32[2,2,4,2048]{3,2,1,0:T(4,128)S(1)} %reshape.38) | data formatting | bytes 262144 | tf_op jit(solution)/shard_map/reshape | solution.py:588
  (9 shorter events, 0.3 us)
Async XLA Ops:
  3.7 1.7 %copy-start.5 = (f32[8,2,12,25,25]{4,1,3,2,0:T(2,128)S(1)}, f32[8,2,12,25,25]{4,1,3,2,0:T(2,128)}, u32[]{:S(2)}) copy-start(f32[8,2,12,25,25]{4,1,3,2,0:T(2,128)} %param.20) | copy-start | bytes 1440004
  5.4 1.1 %copy-start.7 = (f32[2,25,2,12,2,12]{1,4,5,3,2,0:T(2,128)S(1)}, f32[2,25,2,12,2,12]{1,4,5,3,2,0:T(2,128)}, u32[]{:S(2)}) copy-start(f32[2,25,2,12,2,12]{1,4,5,3,2,0:T(2,128)} %param.21) | copy-start | bytes 345604
  5.5 1.1 %copy-start.8 = (f32[2,25,2,12,2,12]{1,4,5,3,2,0:T(2,128)S(1)}, f32[2,25,2,12,2,12]{1,4,5,3,2,0:T(2,128)}, u32[]{:S(2)}) copy-start(f32[2,25,2,12,2,12]{1,4,5,3,2,0:T(2,128)} %param.22) | copy-start | bytes 345604
  5.5 1.2 %copy-start = (s32[2]{0:T(128)S(1)}, s32[2]{0:T(128)}, u32[]{:S(2)}) copy-start(s32[2]{0:T(128)} %box_ref.1) | copy-start | bytes 28
  5.5 1.1 %copy-start.1 = (s32[16]{0:T(128)S(1)}, s32[16]{0:T(128)}, u32[]{:S(2)}) copy-start(s32[16]{0:T(128)} %octant_ref.1) | copy-start | bytes 196
  5.6 1.1 %copy-start.2 = (s32[16]{0:T(128)S(1)}, s32[16]{0:T(128)}, u32[]{:S(2)}) copy-start(s32[16]{0:T(128)} %parent_ref.1) | copy-start | bytes 196
  5.6 1.1 %copy-start.3 = (s32[64]{0:T(128)S(1)}, s32[64]{0:T(128)}, u32[]{:S(2)}) copy-start(s32[64]{0:T(128)} %param.16) | copy-start | bytes 772
  6.7 6.1 %copy-start.10 = (f32[1,2,12,25,25]{4,1,3,2,0:T(2,128)S(1)}, f32[1,2,12,25,25]{4,1,3,2,0:T(2,128)}, u32[]{:S(2)}) copy-start(f32[1,2,12,25,25]{4,1,3,2,0:T(2,128)} %param.23) | copy-start | bytes 180004
  12.8 1.3 %copy-start.6 = (f32[1,2,25,2,32,2,12]{4,5,6,3,2,1,0:T(2,128)S(1)}, f32[1,2,25,2,32,2,12]{4,5,6,3,2,1,0:T(2,128)}, u32[]{:S(2)}) copy-start(f32[1,2,25,2,32,2,12]{4,5,6,3,2,1,0:T(2,128)} %param.24) | copy-start | bytes 921604
  13.1 1.1 %copy-start.9 = (bf16[1,32,25,256]{3,1,2,0:T(8,128)(2,1)S(1)}, bf16[1,32,25,256]{3,1,2,0:T(8,128)(2,1)}, u32[]{:S(2)}) copy-start(bf16[1,32,25,256]{3,1,2,0:T(8,128)(2,1)} %param.26) | copy-start | bytes 1228804
  14.2 0.9 %copy-start.11 = (bf16[64,32,32]{0,2,1:T(8,128)(2,1)S(1)}, bf16[64,32,32]{0,2,1:T(8,128)(2,1)}, u32[]{:S(2)}) copy-start(bf16[64,32,32]{0,2,1:T(8,128)(2,1)} %param.27) | copy-start | bytes 393220
  14.5 0.9 %copy-start.4 = (f32[4]{0:T(128)S(1)}, f32[4]{0:T(128)}, u32[]{:S(2)}) copy-start(f32[4]{0:T(128)} %angle_ref.1) | copy-start | bytes 52

commit v4 on v3

--- a/solution.py
+++ b/solution.py
@@ -132,19 +132,26 @@
     y_ref[...] = jnp.zeros_like(y_ref)
     z_ref[...] = jnp.zeros_like(z_ref)
     rotation_matrices(w_ref, f_ref, orders)
-    slots = xs_ref.shape[1] // 8
+    slots = xs_ref.shape[1]
     cluster = cluster_ref[...]
     code = jnp.full((1, slots), -1, jnp.int32)
     for leaf in range(octant_ref.shape[0]):
         code = jnp.where(cluster == leaf, octant_ref[leaf] * 2 + parent_ref[leaf], code)
     slot = lax.broadcasted_iota(jnp.int32, (1, slots), 1)
     code = jnp.where(slot // (slots // SBLK) < live_ref[0], code, -1)
-    code = jnp.concatenate([code] * 8, axis=1)
-    row = lax.broadcasted_iota(jnp.int32, (128, 8 * slots), 0)
-    col = lax.broadcasted_iota(jnp.int32, (128, 8 * slots), 1) // slots
-    keep = (row // 64 == col // 4) & (row % 4 == col % 4) & ((row % 64) // 4 == code)
-    spread = jnp.where(keep, 1.0, 0.0).astype(jnp.bfloat16)
-    v_ref[...] = dot_nt(xs_ref[...], spread).astype(jnp.bfloat16)
+    place = lax.broadcasted_iota(jnp.int32, (128, slots), 0)
+    spread = jnp.where((place % 64) // 4 == code, 1.0, 0.0).astype(jnp.bfloat16)
+    count = 16 * orders
+    kind = lax.broadcasted_iota(jnp.int32, (count, 128), 0) % 8
+    keep = (kind // 4 == lane // 64) & (kind % 4 == lane % 4)
+    row = lax.broadcasted_iota(jnp.int32, (width, count), 0)
+    col = lax.broadcasted_iota(jnp.int32, (width, count), 1)
+    pick = jnp.where((col // 16 == row % QP) & ((col // 8) % 2 == row // QP), 1.0, 0.0)
+    pick = pick.astype(jnp.bfloat16)
+    for l in range(degrees):
+        r = dot_nt(xs_ref[l * count : (l + 1) * count, :], spread)
+        r = jnp.where(keep, r, 0.0).astype(jnp.bfloat16)
+        v_ref[l * width : (l + 1) * width, :] = dot(pick, r).astype(jnp.bfloat16)
     octant = rep // 2
     box = rep % 2
 
@@ -511,8 +518,7 @@
     bf16 = jnp.bfloat16
     f32 = jnp.float32
 
-    xs = jnp.transpose(sphere_coef, (0, 2, 1, 3, 4, 5)).reshape(degrees, 2, morders, 8 * slots)
-    xs = pad_last(xs, QP, 8 * slots).reshape(degrees * 2 * QP, 8 * slots)
+    xs = sphere_coef.reshape(-1, slots)
     w = jnp.transpose(rotation, (0, 2, 3, 1, 4)).reshape(-1, morders)
     w = jnp.pad(w, ((0, 16), (0, 128 - morders)))
     s1 = axial_rows(jnp.transpose(axial_one, (0, 2, 3, 5, 4, 1)))

time: 40.4 us -> 39.2 us (0.970)
  local copies, waits for them, and re-layouts: 8.92 us -> 6.15 us
  Pallas kernels: 30 us -> 31.7 us
    reshape x2 -> x0, local copies, waits for them, and re-layouts: 3.14 us -> none  [on_device(): jnp.transpose(sphere_coef, (0, 2, 1, 3, 4, 5))]
    pad x1, local copies, waits for them, and re-layouts: 0.16 us -> 1.95 us  [on_device(): w = jnp.pad(w, ((0, 16), (0, 128 - morders)))]
    pallas_call x1, Pallas kernels: 6.05 us -> 7.74 us  [on_device(): pl.pallas_call(functools.partial(local_kernel, morders), out_shape=jax.Sh...]
    unnamed x26, local copies, waits for them, and re-layouts: 4.47 us -> 3.13 us
where the time goes in v4:
time: 39.2 us; the launch traced here: 39 us
  Pallas kernels  31.7 us (81%)
  local copies, waits for them, and re-layouts  6.15 us (16%)
  between operations  0.88 us (2%)
    pallas_call x1, Pallas kernels, on_device(): pl.pallas_call(functools.partial(owner_kernel, dims), out_shape=jax.Shape...  24 us
    pallas_call x1, Pallas kernels, on_device(): pl.pallas_call(functools.partial(local_kernel, morders), out_shape=jax.Sh...  7.74 us
    unnamed x26, local copies, waits for them, and re-layouts  3.13 us
    pad x1, local copies, waits for them, and re-layouts, on_device(): w = jnp.pad(w, ((0, 16), (0, 128 - morders)))  1.95 us
    reshape x2, local copies, waits for them, and re-layouts, on_device(): out = out.reshape(2, 2, 4, PHI)  0.8 us

profile of v4, /device:TPU:0, one launch (start us, length us, event | category | flops | bytes accessed | tf_op | source)
XLA Modules:
  0.0 39.0 jit_solution(15879195079042089399)
XLA Ops:
  0.7 0.0 copy-start.7
  0.7 0.0 copy-start.8
  0.7 1.9 %pad.26.w_ref = f32[4816,128]{1,0:T(8,128)S(1)} pad(f32[4800,25]{1,0:T(8,128)} %bitcast.31, f32[]{:T(128)} %constant.3.clone.1), padding=0_16x0_103 | pad | bytes 2945796 | tf_op jit(solution)/shard_map/jit(_pad)/pad | solution.py:523
  2.6 0.0 copy-start
  2.6 0.0 copy-start.1
  2.6 0.0 copy-start.2
  2.7 0.0 copy-start.3
  2.7 0.0 copy-start.4
  2.7 0.0 copy-done.7
  2.7 0.0 copy-done.8
  2.8 1.1 %copy-done = bf16[12,25,2,2,4,64]{5,4,3,2,1,0:T(4,128)(2,1)S(1)} copy-done((bf16[12,25,2,2,4,64]{5,4,3,2,1,0:T(4,128)(2,1)S(1)}, bf16[12,25,2,2,4,64]{5,4,3,2,1,0:T(4,128)(2,1)}, u32[]{:S(2)}) %copy-start) | copy-done | bytes 614424
  3.9 0.0 copy-done.1
  3.9 0.0 copy-done.2
  3.9 0.0 copy-done.3
  3.9 0.0 copy-done.4
  3.9 0.0 copy-start.10
  3.9 7.7 %shard_map.136.packed_ref = f32[48,128]{1,0:T(8,128)S(1)} custom-call(s32[2]{0:T(128)S(1)} %copy-done.1, s32[1]{0:T(128)S(6)} %copy.24.live_ref, s32[16]{0:T(128)S(1)} %copy-done.2, s32[16]{0:T(128)S(1)} %copy-done.3, bf16[4800,64]{1,0:T(8,128)(2,1)S(1)} %bitcast.29, s32[1,64]{1,0:T(1,128)S(1)} %bitcast.30, f32[4816,128]{1,0:T(8,128)S(1)} %pad.26.w_ref, ...), custom_call_target="tpu_custom_call" | custom-call | tf_op jit(solution)/shard_map/pallas_call | solution.py:528
  11.7 0.0 copy-done.10
  11.7 0.0 copy-start.6
  11.9 0.1 maximum_maximum_fusion.fo_ref
  12.0 0.0 copy-start.9
  12.0 1.0 %copy-done.6 = f32[1,2,25,2,32,2,12]{4,5,6,3,2,1,0:T(2,128)S(1)} copy-done((f32[1,2,25,2,32,2,12]{4,5,6,3,2,1,0:T(2,128)S(1)}, f32[1,2,25,2,32,2,12]{4,5,6,3,2,1,0:T(2,128)}, u32[]{:S(2)}) %copy-start.6) | copy-done | bytes 307224
  13.0 0.1 pad.31.so_ref
  13.1 0.1 copy-done.9
  13.1 0.0 copy-start.11
  13.1 0.2 copy.22
  13.4 0.0 copy-start.5
  13.4 0.6 %copy-done.11 = bf16[64,32,32]{0,2,1:T(8,128)(2,1)S(1)} copy-done((bf16[64,32,32]{0,2,1:T(8,128)(2,1)S(1)}, bf16[64,32,32]{0,2,1:T(8,128)(2,1)}, u32[]{:S(2)}) %copy-start.11) | copy-done | bytes 131096
  14.1 0.1 maximum_convert_fusion.ang_ref
  14.2 0.0 copy-done.5
  14.2 24.0 %shard_map.137 = f32[16,2048]{1,0:T(8,128)S(1)} custom-call(f32[48,128]{1,0:T(8,128)S(1)} %shard_map.136.packed_ref, bf16[12,64,64]{2,1,0:T(8,128)(2,1)S(1)} %maximum_maximum_fusion.fo_ref, f32[2416,128]{1,0:T(8,128)S(1)} %pad.31.so_ref, f32[4]{0:T(128)S(1)} %copy-done.5, bf16[32,32,256]{2,1,0:T(8,128)(2,1)S(1)} %pad.32.turn_ref, ...), custom_call_target="tpu_custom_call" | custom-call | tf_op jit(solution)/shard_map/pallas_call | solution.py:565
  38.3 0.8 %copy.23 = f32[2,2,4,2048]{3,1,0,2:T(2,128)} copy(f32[2,2,4,2048]{3,2,1,0:T(4,128)S(1)} %reshape.34) | data formatting | bytes 262144 | tf_op jit(solution)/shard_map/reshape | solution.py:594
  (9 shorter events, 0.3 us)
Async XLA Ops:
  0.7 2.0 %copy-start.7 = (f32[2,25,2,12,2,12]{1,4,5,3,2,0:T(2,128)S(1)}, f32[2,25,2,12,2,12]{1,4,5,3,2,0:T(2,128)}, u32[]{:S(2)}) copy-start(f32[2,25,2,12,2,12]{1,4,5,3,2,0:T(2,128)} %param.21) | copy-start | bytes 345604
  0.7 2.1 %copy-start.8 = (f32[2,25,2,12,2,12]{1,4,5,3,2,0:T(2,128)S(1)}, f32[2,25,2,12,2,12]{1,4,5,3,2,0:T(2,128)}, u32[]{:S(2)}) copy-start(f32[2,25,2,12,2,12]{1,4,5,3,2,0:T(2,128)} %param.22) | copy-start | bytes 345604
  2.6 1.3 %copy-start = (bf16[12,25,2,2,4,64]{5,4,3,2,1,0:T(4,128)(2,1)S(1)}, bf16[12,25,2,2,4,64]{5,4,3,2,1,0:T(4,128)(2,1)}, u32[]{:S(2)}) copy-start(bf16[12,25,2,2,4,64]{5,4,3,2,1,0:T(4,128)(2,1)} %param.14) | copy-start | bytes 1843204
  2.6 1.3 %copy-start.1 = (s32[2]{0:T(128)S(1)}, s32[2]{0:T(128)}, u32[]{:S(2)}) copy-start(s32[2]{0:T(128)} %box_ref.1) | copy-start | bytes 28
  2.6 1.3 %copy-start.2 = (s32[16]{0:T(128)S(1)}, s32[16]{0:T(128)}, u32[]{:S(2)}) copy-start(s32[16]{0:T(128)} %octant_ref.1) | copy-start | bytes 196
  2.7 1.3 %copy-start.3 = (s32[16]{0:T(128)S(1)}, s32[16]{0:T(128)}, u32[]{:S(2)}) copy-start(s32[16]{0:T(128)} %parent_ref.1) | copy-start | bytes 196
  2.7 1.3 %copy-start.4 = (s32[64]{0:T(128)S(1)}, s32[64]{0:T(128)}, u32[]{:S(2)}) copy-start(s32[64]{0:T(128)} %param.16) | copy-start | bytes 772
  3.9 7.8 %copy-start.10 = (f32[1,2,12,25,25]{4,1,3,2,0:T(2,128)S(1)}, f32[1,2,12,25,25]{4,1,3,2,0:T(2,128)}, u32[]{:S(2)}) copy-start(f32[1,2,12,25,25]{4,1,3,2,0:T(2,128)} %param.23) | copy-start | bytes 180004
  11.7 1.3 %copy-start.6 = (f32[1,2,25,2,32,2,12]{4,5,6,3,2,1,0:T(2,128)S(1)}, f32[1,2,25,2,32,2,12]{4,5,6,3,2,1,0:T(2,128)}, u32[]{:S(2)}) copy-start(f32[1,2,25,2,32,2,12]{4,5,6,3,2,1,0:T(2,128)} %param.24) | copy-start | bytes 921604
  12.0 1.1 %copy-start.9 = (bf16[1,32,25,256]{3,1,2,0:T(8,128)(2,1)S(1)}, bf16[1,32,25,256]{3,1,2,0:T(8,128)(2,1)}, u32[]{:S(2)}) copy-start(bf16[1,32,25,256]{3,1,2,0:T(8,128)(2,1)} %param.26) | copy-start | bytes 1228804
  13.1 0.9 %copy-start.11 = (bf16[64,32,32]{0,2,1:T(8,128)(2,1)S(1)}, bf16[64,32,32]{0,2,1:T(8,128)(2,1)}, u32[]{:S(2)}) copy-start(bf16[64,32,32]{0,2,1:T(8,128)(2,1)} %param.27) | copy-start | bytes 393220
  13.4 0.9 %copy-start.5 = (f32[4]{0:T(128)S(1)}, f32[4]{0:T(128)}, u32[]{:S(2)}) copy-start(f32[4]{0:T(128)} %angle_ref.1) | copy-start | bytes 52
